TPU v7x, 128 devices: a whole 4x4x4 slice. The times are simulated.
128 devices in a mesh: dp: 32 (over y, z, core), ctx: 4 (over x).
Axes of the slice: x: 4, y: 4, z: 4, core: 2. Of those that a mesh axis runs over, the one named last changes fastest.
Arguments:
- tokens: bfloat16 [32, 1024, 4096], P('dp', 'ctx'), may hold values from -40.5 to 40.5
- doc_ids: int32 [32, 1024], P('dp', 'ctx'), may hold values from 0 to 5, never falling along the last dimension, each value on 1 to 512 neighbouring positions
- destinations: int32 [32], replicated, may hold values from 0 to 31, as said below
- norm_gain: float32 [4096], replicated, may hold values from 0.1 to 1.9
- w_query: bfloat16 [4096, 4096], P(None, 'ctx'), may hold values from -1 to 1
- w_key: bfloat16 [4096, 1024], P(None, 'ctx'), may hold values from -1 to 1
- w_value: bfloat16 [4096, 1024], P(None, 'ctx'), may hold values from -0.09375 to 0.09375
- w_out: bfloat16 [4096, 4096], P('ctx'), may hold values from -0.09375 to 0.09375
Outputs:
- attended: bfloat16 [32, 1024, 4096], P('dp', 'ctx')
- kv_cache: bfloat16 [32, 1024, 2048], P('dp', None, 'ctx')
Inputs may be any that keep to these rules, and one draw needn't show every extreme that they name: `doc_ids`: within a packed row the document numbers never fall; a document covers 1 to 512 positions, and some document covers exactly 512. destinations is a permutation of the groups made by sections b = 0, 1, ... up to log2 32 - 1 in order: in section b the two groups whose indices differ only in bit b either exchange the rows they hold or keep them. So before section b a row with anchor g sits at the group whose bits below b are those of destinations[g] and whose other bits are those of g.
All inputs are finite; a program needn't handle non-finite values.
Results may differ from a plain program's by a relative error of at most 0.0083.
Values may be sent and summed in bfloat16 or wider, within the bound.
No kernel may reach another device: no remote copies, remote signals or barrier semaphores. Data moves between devices by JAX's collectives and lax.ppermute only.
A program may use at most 128 MiB of HBM per device.

v0:
```python
import functools
import math

import jax
import jax.numpy as jnp
from jax import lax
from jax.experimental import pallas as pl
from jax.experimental.pallas import tpu as pltpu
from jax.sharding import PartitionSpec as P

HD = 128
VMEM_LIMIT = 60 << 20
PROJECT_WEIGHT = 1
LAST_WEIGHT = 60
ATTEND_WEIGHT = 0


def shifted(value, axis, by):
    count = lax.axis_size(axis)
    return lax.ppermute(value, axis, [(i, (i + by) % count) for i in range(count)])


def normalised(rows, norm_gain):
    wide = rows.astype(jnp.float32)
    scale = lax.rsqrt(jnp.mean(wide * wide, axis=-1, keepdims=True) + 1e-05)
    return (wide * scale * norm_gain).astype(jnp.bfloat16)


def rotary_tables(positions):
    half = HD // 2
    inverse = 500000.0 ** (-2.0 * jnp.arange(half, dtype=jnp.float32) / HD)
    angles = positions[:, None] * inverse
    cosine, sine = jnp.cos(angles), jnp.sin(angles)
    return (
        jnp.concatenate([cosine, cosine], axis=-1),
        jnp.concatenate([-sine, sine], axis=-1),
    )


def project_kernel(plan, *refs):
    rows_ref, held, row_sems, sems = refs[-4:]
    parts = row_sems.shape[0]
    half_refs, refs = refs[:parts], refs[parts:]
    cos_ref, sin_ref, wq_ref, wk_ref, wv_ref = refs[:5]
    if plan is None:
        (out_ref,) = refs[5:6]
    else:
        info_ref, first_ref, own_ref, near_ref = refs[5:9]
        out_ref, pieces_ref, context_ref = refs[9:12]
    half = half_refs[0].shape[0]
    count, _, tile = held.shape
    wide = count - 2

    def source(i):
        if i < 2:
            return (wk_ref, wv_ref)[i]
        return wq_ref.at[:, pl.ds((i - 2) * tile, tile)]

    def start(i):
        pltpu.make_async_copy(source(i), held.at[i], sems.at[i]).start()

    moves = [
        pltpu.make_async_copy(ref, rows_ref.at[pl.ds(i * half, half)], row_sems.at[i])
        for i, ref in enumerate(half_refs)
    ]
    for move in moves:
        move.start()
    start(0)
    start(1)
    for move in moves:
        move.wait()

    def one(i, carry):
        pltpu.make_async_copy(wk_ref, held.at[i], sems.at[i]).wait()
        for k in range(2, count):
            pl.when(i == k - 2)(functools.partial(start, k))
        made = jnp.dot(rows_ref[...], held[i], preferred_element_type=jnp.float32)
        cosine = jnp.where(i == 1, 1.0, cos_ref[...])
        sine = jnp.where(i == 1, 0.0, sin_ref[...])
        slot = jnp.where(i < 2, i + wide, i - 2)
        for at in range(0, tile, HD):
            part = made[:, at : at + HD]
            part = part * cosine + pltpu.roll(part, HD // 2, 1) * sine
            out_ref[slot, :, at : at + HD] = part.astype(out_ref.dtype)
        return carry

    lax.fori_loop(0, count, one, 0)
    if plan is None:
        return
    rows = 2 * half
    kv_refs = [
        own_ref,
        near_ref.at[:, pl.ds(0, rows)],
        near_ref.at[:, pl.ds(rows, rows)],
        out_ref.at[pl.ds(wide, 2)],
    ]
    for kind in (0, 1):
        for slot, kv_ref in enumerate(kv_refs):
            pieces_ref[kind * 16 : (kind + 1) * 16, slot * 16 : (slot + 1) * 16] = kv_ref[
                kind
            ].reshape(16, 16, tile)

    def store(head, block):
        context_ref[:, head * HD : (head + 1) * HD] = block

    attend_quarter(info_ref, first_ref, kv_refs, {plan[1][0][0]: out_ref}, *plan, store)


def project(lot, arrived, tables, w_query, w_key, w_value, earlier=None):
    rows, width = len(arrived) * arrived[0].shape[0], arrived[0].shape[1]
    tile = w_key.shape[1]
    count = 2 + w_query.shape[1] // tile
    anywhere = pl.BlockSpec(memory_space=pl.ANY)
    table = pl.BlockSpec((pl.Element(rows), pl.Element(HD)), lambda i: (lot, 0))
    whole = lambda shape: pl.BlockSpec(shape, lambda i: (0,) * len(shape))
    operands = [*arrived, *tables, w_query, w_key, w_value]
    in_specs = [anywhere] * len(arrived) + [table] * 2 + [anywhere] * 3
    shapes = [(count, rows, tile)]
    plan, weight = None, PROJECT_WEIGHT
    if earlier is not None:
        info, first_wide, made, plan = earlier
        operands += [info, first_wide, *made]
        in_specs += [pl.BlockSpec(memory_space=pltpu.SMEM), whole(first_wide.shape)]
        in_specs += [
            pl.BlockSpec((2, m.shape[1], tile), lambda i: (count // 2 - 1, 0, 0)) for m in made
        ]
        shapes += [(32, 64, tile), (rows, (count - 2) * tile)]
        weight = LAST_WEIGHT
    return pl.pallas_call(
        functools.partial(project_kernel, plan),
        grid=(1,),
        in_specs=in_specs,
        out_specs=[whole(shape) for shape in shapes],
        out_shape=[jax.ShapeDtypeStruct(shape, jnp.bfloat16) for shape in shapes],
        scratch_shapes=[
            pltpu.VMEM((rows, width), jnp.bfloat16),
            pltpu.VMEM((count, width, tile), jnp.bfloat16),
            pltpu.SemaphoreType.DMA((len(arrived),)),
            pltpu.SemaphoreType.DMA((count,)),
        ],
        compiler_params=pltpu.CompilerParams(vmem_limit_bytes=VMEM_LIMIT),
        cost_estimate=pl.CostEstimate(
            flops=weight * 2 * rows * width * tile * count,
            bytes_accessed=2 * width * (tile * count + rows),
            transcendentals=0,
        ),
        name="project" if earlier is None else "project_attend",
    )(*operands)


def attend_quarter(info_ref, first_ref, kv_refs, q_refs, slots, q_slots, store):
    blocks, base = info_ref[0], info_ref[1]
    half = first_ref.shape[0] // 8
    rows = 2 * half
    factor = math.log2(math.e) / math.sqrt(HD)
    first = jnp.concatenate(
        [first_ref[lot * rows + at : lot * rows + at + half, :1] for lot, at in q_slots], axis=0
    )

    def run(used):
        count = used * rows
        column = lax.broadcasted_iota(jnp.int32, (rows, count), 1) + (base + rows - count)
        line = lax.broadcasted_iota(jnp.int32, (rows, count), 0) + base
        bias = jnp.where((column >= first) & (column <= line), 0.0, -1e30)
        ones = jnp.ones((count, HD), jnp.bfloat16)
        pieces = slots[2 * (3 - used) :]
        for kv_head in range(2):
            place = slice(kv_head * HD, (kv_head + 1) * HD)
            keys = jnp.concatenate([kv_refs[a][0, at : at + half, place] for a, at in pieces], axis=0)
            values = jnp.concatenate(
                [kv_refs[a][1, at : at + half, place] for a, at in pieces], axis=0
            )
            values = jnp.concatenate([values, ones], axis=1)
            for head in range(4 * kv_head, 4 * kv_head + 4):
                within = slice(head % 2 * HD, (head % 2 + 1) * HD)
                queries = jnp.concatenate(
                    [q_refs[a][head // 2, at : at + half, within] for a, at in q_slots], axis=0
                )
                scores = lax.dot_general(
                    queries, keys, (((1,), (1,)), ((), ())), preferred_element_type=jnp.float32
                )
                scores = scores + bias
                most = jnp.max(scores, axis=-1, keepdims=True)
                weights = jnp.exp2((scores - most) * factor).astype(jnp.bfloat16)
                summed = jnp.dot(weights, values, preferred_element_type=jnp.float32)
                store(head, (summed[:, :HD] / summed[:, HD:]).astype(jnp.bfloat16))

    for used in (1, 2, 3):
        pl.when(blocks == used)(functools.partial(run, used))


def attend_kernel(plan, lots, with_own, *refs):
    quarters = len(plan)
    info_refs, first_ref = refs[:quarters], refs[quarters]
    own_ref, near_ref, far_ref = refs[quarters + 1 : quarters + 4]
    rows = own_ref.shape[1]
    kv_refs = [own_ref, near_ref.at[:, pl.ds(0, rows)], near_ref.at[:, pl.ds(rows, rows)], far_ref]
    refs = refs[quarters + 4 :]
    q_refs = dict(zip(lots, refs))
    refs = refs[len(lots) :]
    if with_own:
        w_ref, out_ref, context, held, sems = refs
        tile = held.shape[2]
        copies = [
            pltpu.make_async_copy(w_ref.at[:, pl.ds(i * tile, tile)], held.at[i], sems.at[i])
            for i in range(held.shape[0])
        ]
        for copy in copies:
            copy.start()
        out_refs = [context]
    else:
        out_refs = refs[:quarters]
    for info_ref, out_ref_e, (slots, q_slots) in zip(info_refs, out_refs, plan):

        def store(head, block, out_ref_e=out_ref_e):
            out_ref_e[:, head * HD : (head + 1) * HD] = block

        attend_quarter(info_ref, first_ref, kv_refs, q_refs, slots, q_slots, store)
    if with_own:
        for i, copy in enumerate(copies):
            copy.wait()
            out_ref[:, i * tile : (i + 1) * tile] = jnp.dot(
                context[...], held[i], preferred_element_type=jnp.float32
            )


def attend(infos, first_wide, made, plan, w_out=None):
    count, rows, tile = made[0].shape
    width = (count - 2) * tile
    lots = sorted({a for _, q_slots in plan for a, _ in q_slots})
    spots = [((0, 0), (1, 0), (1, 1), (2, 0))[lot] for lot in lots]
    smem = pl.BlockSpec(memory_space=pltpu.SMEM)
    whole = lambda shape: pl.BlockSpec(shape, lambda i: (0,) * len(shape))
    in_specs = (
        [smem] * len(plan)
        + [whole(first_wide.shape)]
        + [pl.BlockSpec((2, m.shape[1], tile), lambda i: (count // 2 - 1, 0, 0)) for m in made]
        + [
            pl.BlockSpec((count - 2, rows, tile), functools.partial(lambda n, i: (0, n, 0), spot))
            for _, spot in spots
        ]
    )
    operands = [*infos, first_wide, *made, *[made[a] for a, _ in spots]]
    scratch = []
    if w_out is None:
        shapes = [jax.ShapeDtypeStruct((rows, width), jnp.bfloat16)] * len(plan)
    else:
        in_specs.append(pl.BlockSpec(memory_space=pl.ANY))
        operands.append(w_out)
        shapes = [jax.ShapeDtypeStruct((rows, w_out.shape[1]), jnp.float32)]
        scratch = [
            pltpu.VMEM((rows, width), jnp.bfloat16),
            pltpu.VMEM((4, width, w_out.shape[1] // 4), jnp.bfloat16),
            pltpu.SemaphoreType.DMA((4,)),
        ]
    return pl.pallas_call(
        functools.partial(attend_kernel, plan, lots, w_out is not None),
        grid=(1,),
        in_specs=in_specs,
        out_specs=[whole(shape.shape) for shape in shapes],
        out_shape=shapes,
        scratch_shapes=scratch,
        compiler_params=pltpu.CompilerParams(vmem_limit_bytes=VMEM_LIMIT),
        cost_estimate=pl.CostEstimate(
            flops=ATTEND_WEIGHT * 12 * len(plan) * rows * rows * width,
            bytes_accessed=2 * (2 * rows * width + 3 * made[0].size),
            transcendentals=0,
        ),
        name="attend",
    )(*operands)


def others_kernel(order, *refs):
    count = len(order)
    context_refs = refs[:count]
    w_ref, partial_ref, out_ref, held, sums, stacked, sems, sum_sems, context_sems = refs[count:]
    slots, _, tile = held.shape
    depth = w_ref.shape[1]
    steps = out_ref.shape[1] // tile

    def copies(step, slot):
        at = pl.multiple_of(step * tile, tile)
        return [
            pltpu.make_async_copy(
                w_ref.at[index, :, pl.ds(at, tile)],
                held.at[slot, pl.ds(i * depth, depth)],
                sems.at[slot, i],
            )
            for i, index in enumerate(order)
        ] + [
            pltpu.make_async_copy(
                partial_ref.at[:, pl.ds(at, tile)], sums.at[slot], sum_sems.at[slot]
            )
        ]

    gathers = [
        pltpu.make_async_copy(
            ref, stacked.at[:, pl.ds(i * depth, depth)], context_sems.at[i]
        )
        for i, ref in enumerate(context_refs)
    ]
    for gather in gathers:
        gather.start()
    for step in range(slots - 1):
        for copy in copies(step, step):
            copy.start()
    for gather in gathers:
        gather.wait()

    def one(step, carry):
        slot = lax.rem(step, slots)
        for copy in copies(step, slot):
            copy.wait()

        @pl.when(step + slots - 1 < steps)
        def _():
            for copy in copies(step + slots - 1, lax.rem(step + slots - 1, slots)):
                copy.start()

        total = sums[slot] + jnp.dot(
            stacked[...], held[slot], preferred_element_type=jnp.float32
        )
        out_ref[:, pl.ds(pl.multiple_of(step * tile, tile), tile)] = total.astype(out_ref.dtype)
        return carry

    lax.fori_loop(0, steps, one, 0)


def other_terms(contexts, order, others, partial):
    rows, depth = contexts[0].shape
    width = others.shape[-1]
    tile, slots, count = 512, 3, len(contexts)
    anywhere = pl.BlockSpec(memory_space=pl.ANY)
    return pl.pallas_call(
        functools.partial(others_kernel, order),
        grid=(1,),
        in_specs=[anywhere] * (count + 2),
        out_specs=pl.BlockSpec((rows, width), lambda i: (0, 0)),
        out_shape=jax.ShapeDtypeStruct((rows, width), jnp.bfloat16),
        scratch_shapes=[
            pltpu.VMEM((slots, count * depth, tile), jnp.bfloat16),
            pltpu.VMEM((slots, rows, tile), jnp.float32),
            pltpu.VMEM((rows, count * depth), jnp.bfloat16),
            pltpu.SemaphoreType.DMA((slots, count)),
            pltpu.SemaphoreType.DMA((slots,)),
            pltpu.SemaphoreType.DMA((count,)),
        ],
        compiler_params=pltpu.CompilerParams(vmem_limit_bytes=VMEM_LIMIT),
        cost_estimate=pl.CostEstimate(
            flops=2 * count * rows * depth * width,
            bytes_accessed=2 * count * depth * width,
            transcendentals=0,
        ),
        name="other_terms",
    )(*contexts, others, partial)


def reorder_kernel(source_ref, in_ref, out_ref):
    def one(i, carry):
        out_ref[i] = in_ref[source_ref[i]]
        return carry

    lax.fori_loop(0, in_ref.shape[0], one, 0)


def routed(pieces, source, after):
    scattered = lax.all_to_all(pieces, "dp", 0, 0, tiled=False)
    scattered, after = lax.optimization_barrier((scattered, after))
    whole = pl.BlockSpec(pieces.shape, lambda i: (0, 0, 0))
    ordered = pl.pallas_call(
        reorder_kernel,
        grid=(1,),
        in_specs=[pl.BlockSpec(memory_space=pltpu.SMEM), whole],
        out_specs=whole,
        out_shape=jax.ShapeDtypeStruct(pieces.shape, pieces.dtype),
        name="reorder",
    )(source, scattered)
    return lax.all_to_all(ordered, "dp", 0, 0, tiled=False), after


def assemble_kernel(spots, place_ref, pieces_ref, out_ref):
    quarters = len(spots) // 2
    rows = out_ref.shape[0] // quarters
    half = rows // 2
    for quarter in range(quarters):
        base = pl.multiple_of(lax.rem(place_ref[0] + quarter, quarters) * rows, rows)
        for which in (0, 1):
            slot, at = spots[2 * quarter + which]
            for kind in range(2):
                block = pieces_ref[
                    kind * 16 + at // 16 : kind * 16 + (at + half) // 16,
                    slot * 16 : (slot + 1) * 16,
                ].reshape(half, 2 * HD)
                for head in range(2):
                    to = (2 * head + kind) * HD
                    out_ref[pl.ds(base + which * half, half), to : to + HD] = block[
                        :, head * HD : (head + 1) * HD
                    ]


def assemble(spots, place, pieces, shape):
    whole = lambda shape: pl.BlockSpec(shape, lambda i: (0,) * len(shape))
    return pl.pallas_call(
        functools.partial(assemble_kernel, spots),
        grid=(1,),
        in_specs=[pl.BlockSpec(memory_space=pltpu.SMEM), whole(pieces.shape)],
        out_specs=whole(shape),
        out_shape=jax.ShapeDtypeStruct(shape, pieces.dtype),
        name="assemble",
    )(jnp.reshape(place, (1,)).astype(jnp.int32), pieces)


def shards(tokens, doc_ids, destinations, norm_gain, w_query, w_key, w_value, w_out):
    quarters = lax.axis_size("ctx")
    groups = lax.axis_size("dp")
    place = lax.axis_index("ctx")
    row = lax.axis_index("dp")
    rows = tokens.shape[1]
    half = rows // 2

    ids = [doc_ids[0]] + [shifted(doc_ids[0], "ctx", -e) for e in range(1, quarters)]

    share = w_out.shape[0] // groups
    mine = lax.dynamic_slice_in_dim(w_out, row * share, share, 0)
    shares = jnp.stack([shifted(mine, "ctx", e) for e in range(1, quarters)])

    normed = normalised(tokens[0], norm_gain)
    low, high = normed[:half], normed[half:]
    halves = [((0, 0), (0, 1)), ((1, 1), (3, 0)), ((1, 0), (3, 1)), ((2, 0), (2, 1))]
    where = {h: (i, j * half) for i, pair in enumerate(halves) for j, h in enumerate(pair)}

    bases = [(place + e) % quarters * rows for e in range(quarters)]
    steps = jnp.arange(half, dtype=jnp.int32)
    order = [h for pair in halves for h in pair]
    row_index = jnp.concatenate([bases[q] + (h * half + steps) for q, h in order])
    row_ids = jnp.concatenate([ids[q][h * half : (h + 1) * half] for q, h in order])
    first = jnp.min(
        jnp.where(row_ids[:, None] == row_ids[None, :], row_index[None, :], quarters * rows), axis=-1
    )
    cosine, sine = rotary_tables((row_index - first).astype(jnp.float32))
    first_wide = jnp.broadcast_to(first[:, None], (first.shape[0], HD))
    infos = []
    for e in range(quarters):
        lot, at = where[(e, 0)]
        least = first[lot * rows + at]
        count = 1 + (least < bases[e]).astype(jnp.int32) + (least < bases[e] - rows).astype(jnp.int32)
        infos.append(jnp.stack([count, bases[e]]))
    cosine, sine, first_wide, infos = lax.optimization_barrier((cosine, sine, first_wide, infos))

    before_low, after_high = shifted(low, "ctx", 1), shifted(high, "ctx", -1)
    then_low, then_high, _ = lax.optimization_barrier((low, high, first))
    before_high, after_low = shifted(then_high, "ctx", 1), shifted(then_low, "ctx", -1)
    far_low, far_high = shifted(before_low, "ctx", 1), shifted(after_high, "ctx", -1)
    low, high, shares = lax.optimization_barrier((low, high, shares))
    others = lax.all_gather(shares, "dp", axis=1, tiled=True)
    lots = [(low, high), (after_high, before_low), (after_low, before_high), (far_low, far_high)]

    plan = [
        (
            [where[(q % quarters, h)] for q in (e - 2, e - 1, e) for h in (0, 1)],
            [where[(e, h)] for h in (0, 1)],
        )
        for e in range(quarters)
    ]
    weights = (w_query, w_key, w_value)
    tables = (cosine, sine)
    made = [
        project(0, lots[0], tables, *weights),
        project(rows, lots[1] + lots[2], tables, *weights),
    ]
    made = [m[0] for m in made]
    last, pieces, opposite = project(
        3 * rows, lots[3], tables, *weights, (infos[2], first_wide, made, plan[2])
    )
    made.append(last)
    after, before = attend([infos[1], infos[3]], first_wide, made, [plan[1], plan[3]])
    received = [shifted(c, "ctx", e) for c, e in ((opposite, 2), (after, 1), (before, 3))]
    (partial,) = attend([infos[0]], first_wide, made, [plan[0]], w_out)

    anchors = jnp.arange(groups, dtype=jnp.int32)
    source = jnp.sum(jnp.where(destinations[None, :] == anchors[:, None], anchors[None, :], 0), axis=1)
    delivered, partial = routed(pieces, source, partial)
    attended = other_terms(received, (1, 0, 2), others, partial)
    delivered, attended = lax.optimization_barrier((delivered, attended))
    spots = tuple(where[(q, h)] for q in range(quarters) for h in (0, 1))
    shape = (quarters * rows, w_key.shape[1] + w_value.shape[1])
    kv_cache = assemble(spots, place, delivered, shape)
    return attended[None], kv_cache[None]


def solution(mesh):
    return jax.shard_map(
        shards,
        mesh=mesh,
        in_specs=(
            P("dp", "ctx", None),
            P("dp", "ctx"),
            P(),
            P(),
            P(None, "ctx"),
            P(None, "ctx"),
            P(None, "ctx"),
            P("ctx", None),
        ),
        out_specs=(P("dp", "ctx", None), P("dp", None, "ctx")),
        check_vma=False,
    )
```

profile of v0, /device:TPU:1, one launch (start us, length us, event | category | flops | bytes accessed | tf_op | source)
XLA Modules:
  0.0 186.5 jit_solution(4673703013027907241)
XLA Ops:
  8.2 3.4 %collective-permute-start.9 = (bf16[32,4096]{1,0:T(8,128)(2,1)S(1)}, bf16[32,4096]{1,0:T(8,128)(2,1)S(1)}, u32[]{:S(2)}, u32[]{:S(2)}) collective-permute-start(bf16[32,4096]{1,0:T(8,128)(2,1)S(1)} %constant_dynamic-slice_fusion), channel_id=1, source_target_pairs={{0,3},{1,0},{2,1},{3,2},{4,7},{5,4},{6,5},{7,6},{8,11},{9,8},{10,9... | collective-permute-start | bytes 786440 | tf_op jit(solution)/shard_map/ppermute | solution.py:20
  12.7 2.1 %fusion = f32[256]{0:T(256)S(1)} fusion(bf16[1,256,4096]{2,1,0:T(8,128)(2,1)} %param.8), kind=kLoop, calls=%fused_computation.2 | loop fusion | flops 3145472 | bytes 2098176 | tf_op jit(solution)/shard_map/reduce_sum | solution.py:25
  14.8 2.2 %fusion.2 = bf16[256,4096]{1,0:T(8,128)(2,1)S(1)} fusion(bf16[1,256,4096]{2,1,0:T(8,128)(2,1)} %param.8, f32[4096]{0:T(1024)} %param.11, f32[256]{0:T(256)S(1)} %add_rsqrt_fusion), kind=kLoop, calls=%fused_computation.4 | loop fusion | flops 4194304 | bytes 4211712 | tf_op jit(solution)/shard_map/convert_element_type | solution.py:26
  17.7 2.2 %collective-permute-done.8 = bf16[32,4096]{1,0:T(8,128)(2,1)S(1)} collective-permute-done((bf16[32,4096]{1,0:T(8,128)(2,1)S(1)}, bf16[32,4096]{1,0:T(8,128)(2,1)S(1)}, u32[]{:S(2)}, u32[]{:S(2)}) %collective-permute-start.8) | collective-permute-done | bytes 262176 | tf_op jit(solution)/shard_map/ppermute | solution.py:20
  20.0 6.9 %collective-permute-done.7 = bf16[32,4096]{1,0:T(8,128)(2,1)S(1)} collective-permute-done((bf16[32,4096]{1,0:T(8,128)(2,1)S(1)}, bf16[32,4096]{1,0:T(8,128)(2,1)S(1)}, u32[]{:S(2)}, u32[]{:S(2)}) %collective-permute-start.7) | collective-permute-done | bytes 262176 | tf_op jit(solution)/shard_map/ppermute | solution.py:20
  28.1 2.7 %collective-permute-start.2 = (bf16[128,4096]{1,0:T(8,128)(2,1)S(1)}, bf16[128,4096]{1,0:T(8,128)(2,1)}, u32[]{:S(2)}, u32[]{:S(2)}) collective-permute-start(bf16[128,4096]{1,0:T(8,128)(2,1)S(1)} %get-tuple-element.30.refs_1_), channel_id=1, source_target_pairs={{0,3},{1,0},{2,1},{3,2},{4,7},{5,4},{6,5},{7,6},{8,11},{9,8},{10,9... | collective-permute-start | bytes 3145736 | tf_op jit(solution)/shard_map/ppermute | solution.py:20
  32.4 20.1 %collective-permute-done.4 = s32[256]{0:T(256)S(1)} collective-permute-done((s32[256]{0:T(256)S(1)}, s32[256]{0:T(256)S(1)}, u32[]{:S(2)}, u32[]{:S(2)}) %collective-permute-start.4) | collective-permute-done | bytes 1056 | tf_op jit(solution)/shard_map/ppermute | solution.py:20
  57.5 2.4 %collective-permute-start.10 = (bf16[128,4096]{1,0:T(8,128)(2,1)S(1)}, bf16[128,4096]{1,0:T(8,128)(2,1)}, u32[]{:S(2)}, u32[]{:S(2)}) collective-permute-start(bf16[128,4096]{1,0:T(8,128)(2,1)S(1)} %get-tuple-element.29.refs_0_), channel_id=1, source_target_pairs={{0,3},{1,0},{2,1},{3,2},{4,7},{5,4},{6,5},{7,6},{8,11},{9,8},{10,9... | collective-permute-start | bytes 3145736 | tf_op jit(solution)/shard_map/ppermute | solution.py:20
  63.0 1.9 %fusion.3 = (f32[1024,64]{1,0:T(8,128)S(1)}, f32[1024,64]{1,0:T(8,128)S(1)}, f32[1024,64]{1,0:T(8,128)S(1)}) fusion(f32[64]{0:T(128)S(1)} %multiply_power_fusion, f32[1024]{0:T(1024)S(1)} %subtract_convert_fusion), kind=kLoop, calls=%fused_computation.11 | loop fusion | flops 131072 | bytes 790784 | tf_op jit(solution)/shard_map/neg | solution.py:36
  65.0 2.7 %collective-permute-start.3 = (bf16[128,4096]{1,0:T(8,128)(2,1)}, bf16[128,4096]{1,0:T(8,128)(2,1)}, u32[]{:S(2)}, u32[]{:S(2)}) collective-permute-start(bf16[128,4096]{1,0:T(8,128)(2,1)} %collective-permute-done.2.refs_0_), channel_id=1, source_target_pairs={{0,3},{1,0},{2,1},{3,2},{4,7},{5,4},{6,5},{7,6},{8,11},{9,8},{10,9... | collective-permute-start | bytes 3145736 | tf_op jit(solution)/shard_map/ppermute | solution.py:20
  70.8 10.0 %project.2.refs_9_.refs_2_.refs_5_.refs_3_ = bf16[6,256,256]{2,1,0:T(8,128)(2,1)} custom-call(bf16[128,4096]{1,0:T(8,128)(2,1)} %copy-done.3, bf16[128,4096]{1,0:T(8,128)(2,1)} %copy-done.2, f32[1024,128]{1,0:T(8,128)} %get-tuple-element.23.refs_2_.refs_4_, f32[1024,128]{1,0:T(8,128)} %get-tuple-element.24.refs_3_.refs_5_, bf16[4096,1024]{1,0:T(8,128)(2,1)} %refs_4_.3, ...), custom_call_target="tpu_custom_call" | custom-call | flops 3221225472 | bytes 14680064 | tf_op jit(solution)/shard_map/project/pallas_call | solution.py:129
  81.0 2.9 %collective-permute-done.11.refs_3_ = bf16[128,4096]{1,0:T(8,128)(2,1)} collective-permute-done((bf16[128,4096]{1,0:T(8,128)(2,1)S(1)}, bf16[128,4096]{1,0:T(8,128)(2,1)}, u32[]{:S(2)}, u32[]{:S(2)}) %collective-permute-start.11) | collective-permute-done | bytes 1048608 | tf_op jit(solution)/shard_map/ppermute | solution.py:20
  83.9 13.2 %project.3.refs_10_.refs_3_.refs_4_.refs_6_.refs_7_ = bf16[6,512,256]{2,1,0:T(8,128)(2,1)} custom-call(bf16[128,4096]{1,0:T(8,128)(2,1)} %collective-permute-done.2.refs_0_, bf16[128,4096]{1,0:T(8,128)(2,1)} %copy-done.7, bf16[128,4096]{1,0:T(8,128)(2,1)} %collective-permute-done.10.refs_2_, bf16[128,4096]{1,0:T(8,128)(2,1)} %collective-permute-done.11.refs_3_, ...), custom_call_target="tpu_custom_call" | custom-call | flops 6442450944 | bytes 16777216 | tf_op jit(solution)/shard_map/project/pallas_call | solution.py:129
  97.2 9.2 %collective-permute-done.1.refs_0_ = bf16[128,4096]{1,0:T(8,128)(2,1)} collective-permute-done((bf16[128,4096]{1,0:T(8,128)(2,1)S(1)}, bf16[128,4096]{1,0:T(8,128)(2,1)}, u32[]{:S(2)}, u32[]{:S(2)}) %collective-permute-start.1) | collective-permute-done | bytes 1048608 | tf_op jit(solution)/shard_map/ppermute | solution.py:20
  106.4 11.4 %project_attend.1 = (bf16[6,256,256]{2,1,0:T(8,128)(2,1)}, bf16[32,64,256]{2,1,0:T(8,128)(2,1)}, bf16[256,1024]{1,0:T(8,128)(2,1)}) custom-call(bf16[128,4096]{1,0:T(8,128)(2,1)} %collective-permute-done.1.refs_0_, bf16[128,4096]{1,0:T(8,128)(2,1)} %collective-permute-done.3.refs_1_, f32[1024,128]{1,0:T(8,128)} %get-tuple-element.23.refs_2_.refs_4_, ...), custom_call_target="tpu_custom_call" | custom-call | flops 193273528320 | bytes 14680064 | tf_op jit(solution)/shard_map/project_attend/pallas_call | solution.py:129
  117.9 12.6 %all-to-all-start = ((bf16[32,64,256]{2,1,0:T(8,128)(2,1)}), bf16[32,64,256]{2,1,0:T(8,128)(2,1)S(1)}, u32[]{:S(2)}, u32[]{:S(2)}) async-start(bf16[32,64,256]{2,1,0:T(8,128)(2,1)} %get-tuple-element.31), calls=%async_computation | async-start | bytes 2097152 | tf_op jit(solution)/shard_map/all_to_all | solution.py:367
  130.6 6.2 %attend.3 = (bf16[256,1024]{1,0:T(8,128)(2,1)}, bf16[256,1024]{1,0:T(8,128)(2,1)}) custom-call(s32[2]{0:T(128)} %get-tuple-element.36.refs_0_, s32[2]{0:T(128)} %get-tuple-element.37.refs_1_, s32[1024,128]{1,0:T(8,128)} %broadcast_in_dim.50.refs_8_.refs_1_.refs_2_, bf16[6,256,256]{2,1,0:T(8,128)(2,1)} %project.2.refs_9_.refs_2_.refs_5_.refs_3_, ...), custom_call_target="tpu_custom_call" | custom-call | bytes 3407872 | tf_op jit(solution)/shard_map/attend/pallas_call | solution.py:256
  136.8 2.7 %collective-permute-start.14 = (bf16[256,1024]{1,0:T(8,128)(2,1)}, bf16[256,1024]{1,0:T(8,128)(2,1)S(1)}, u32[]{:S(2)}, u32[]{:S(2)}) collective-permute-start(bf16[256,1024]{1,0:T(8,128)(2,1)} %get-tuple-element.39), channel_id=1, source_target_pairs={{0,3},{1,0},{2,1},{3,2},{4,7},{5,4},{6,5},{7,6},{8,11},{9,8},{10,9... | collective-permute-start | bytes 1572872 | tf_op jit(solution)/shard_map/ppermute | solution.py:20
  140.1 7.9 %attend.2.refs_4_ = f32[256,4096]{1,0:T(8,128)} custom-call(s32[2]{0:T(128)} %get-tuple-element.32.refs_0_, s32[1024,128]{1,0:T(8,128)} %broadcast_in_dim.50.refs_8_.refs_1_.refs_2_, bf16[6,256,256]{2,1,0:T(8,128)(2,1)} %project.2.refs_9_.refs_2_.refs_5_.refs_3_, bf16[6,512,256]{2,1,0:T(8,128)(2,1)} %project.3.refs_10_.refs_3_.refs_4_.refs_6_.refs_7_, ...), custom_call_target="tpu_custom_call" | custom-call | bytes 3407872 | tf_op jit(solution)/shard_map/attend/pallas_call | solution.py:256
  149.0 2.4 %reorder.1 = bf16[32,64,256]{2,1,0:T(8,128)(2,1)} custom-call(s32[32]{0:T(128)} %select_reduce_fusion.1.source_ref, bf16[32,64,256]{2,1,0:T(8,128)(2,1)} %copy-done), custom_call_target="tpu_custom_call" | custom-call | tf_op jit(solution)/shard_map/reorder/pallas_call | solution.py:370
  151.5 7.9 %all-to-all-start.1 = ((bf16[32,64,256]{2,1,0:T(8,128)(2,1)}), bf16[32,64,256]{2,1,0:T(8,128)(2,1)S(1)}, u32[]{:S(2)}, u32[]{:S(2)}) async-start(bf16[32,64,256]{2,1,0:T(8,128)(2,1)} %reorder.1), calls=%async_computation.1 | async-start | bytes 2097152 | tf_op jit(solution)/shard_map/all_to_all | solution.py:378
  160.6 13.3 %other_terms.1 = bf16[256,4096]{1,0:T(8,128)(2,1)} custom-call(bf16[256,1024]{1,0:T(8,128)(2,1)} %copy-done.4, bf16[256,1024]{1,0:T(8,128)(2,1)} %copy-done.5, bf16[256,1024]{1,0:T(8,128)(2,1)} %copy-done.6, bf16[3,1024,4096]{2,1,0:T(8,128)(2,1)} %all-gather.2.cloned.1.call-done.refs_3_, f32[256,4096]{1,0:T(8,128)} %attend.2.refs_4_), custom_call_target="tpu_custom_call" | custom-call | flops 6442450944 | bytes 25165824 | tf_op jit(solution)/shard_map/other_terms/pallas_call | solution.py:334
  173.9 2.4 %all-to-all-done.1.pieces_ref = bf16[32,64,256]{2,1,0:T(8,128)(2,1)S(1)} async-done(((bf16[32,64,256]{2,1,0:T(8,128)(2,1)}), bf16[32,64,256]{2,1,0:T(8,128)(2,1)S(1)}, u32[]{:S(2)}, u32[]{:S(2)}) %all-to-all-start.1) | async-done | bytes 1048608 | tf_op jit(solution)/shard_map/all_to_all | solution.py:378
  177.3 2.3 %assemble.1 = bf16[1024,512]{1,0:T(8,128)(2,1)} custom-call(s32[1]{0:T(128)} %bitcast.21.place_ref, bf16[32,64,256]{2,1,0:T(8,128)(2,1)} %copy-done.1), custom_call_target="tpu_custom_call" | custom-call | tf_op jit(solution)/shard_map/assemble/pallas_call | solution.py:403
  (74 shorter events, 15.7 us)
Async XLA Ops:
  7.2 152.4 %all-gather.2.cloned.1.call-start = ((), (), s32[]{:S(2)}) async-start(), calls=%async_computation.2 | async-start | bytes 25952256 | tf_op jit(solution)/shard_map/all_gather | solution.py:455
  8.2 9.6 %collective-permute-start.9 = (bf16[32,4096]{1,0:T(8,128)(2,1)S(1)}, bf16[32,4096]{1,0:T(8,128)(2,1)S(1)}, u32[]{:S(2)}, u32[]{:S(2)}) collective-permute-start(bf16[32,4096]{1,0:T(8,128)(2,1)S(1)} %constant_dynamic-slice_fusion), channel_id=1, source_target_pairs={{0,3},{1,0},{2,1},{3,2},{4,7},{5,4},{6,5},{7,6},{8,11},{9,8},{10,9... | collective-permute-start | bytes 786440 | tf_op jit(solution)/shard_map/ppermute | solution.py:20
  11.6 8.4 %collective-permute-start.8 = (bf16[32,4096]{1,0:T(8,128)(2,1)S(1)}, bf16[32,4096]{1,0:T(8,128)(2,1)S(1)}, u32[]{:S(2)}, u32[]{:S(2)}) collective-permute-start(bf16[32,4096]{1,0:T(8,128)(2,1)S(1)} %constant_dynamic-slice_fusion), channel_id=1, source_target_pairs={{0,2},{1,3},{2,0},{3,1},{4,6},{5,7},{6,4},{7,5},{8,10},{9,11},{10,... | collective-permute-start | bytes 786440 | tf_op jit(solution)/shard_map/ppermute | solution.py:20
  12.1 14.8 %collective-permute-start.7 = (bf16[32,4096]{1,0:T(8,128)(2,1)S(1)}, bf16[32,4096]{1,0:T(8,128)(2,1)S(1)}, u32[]{:S(2)}, u32[]{:S(2)}) collective-permute-start(bf16[32,4096]{1,0:T(8,128)(2,1)S(1)} %constant_dynamic-slice_fusion), channel_id=1, source_target_pairs={{0,1},{1,2},{2,3},{3,0},{4,5},{5,6},{6,7},{7,4},{8,9},{9,10},{10,1... | collective-permute-start | bytes 786440 | tf_op jit(solution)/shard_map/ppermute | solution.py:20
  17.0 13.7 %copy-start.8 = (s32[1,256]{1,0:T(1,128)S(1)}, s32[1,256]{1,0:T(1,128)}, u32[]{:S(2)}) copy-start(s32[1,256]{1,0:T(1,128)} %param.9) | copy-start | bytes 3076
  17.2 53.6 %copy-start.2 = (bf16[128,4096]{1,0:T(8,128)(2,1)}, bf16[128,4096]{1,0:T(8,128)(2,1)S(1)}, u32[]{:S(2)}) copy-start(bf16[128,4096]{1,0:T(8,128)(2,1)S(1)} %get-tuple-element.30.refs_1_) | copy-start | bytes 3145732
  17.2 53.6 %copy-start.3 = (bf16[128,4096]{1,0:T(8,128)(2,1)}, bf16[128,4096]{1,0:T(8,128)(2,1)S(1)}, u32[]{:S(2)}) copy-start(bf16[128,4096]{1,0:T(8,128)(2,1)S(1)} %get-tuple-element.29.refs_0_) | copy-start | bytes 3145732
  28.0 37.0 %collective-permute-start = (bf16[128,4096]{1,0:T(8,128)(2,1)S(1)}, bf16[128,4096]{1,0:T(8,128)(2,1)S(1)}, u32[]{:S(2)}, u32[]{:S(2)}) collective-permute-start(bf16[128,4096]{1,0:T(8,128)(2,1)S(1)} %get-tuple-element.29.refs_0_), channel_id=1, source_target_pairs={{0,1},{1,2},{2,3},{3,0},{4,5},{5,6},{6,7},{7,4},{8,9},{9,10},{10,1... | collective-permute-start | bytes 3145736 | tf_op jit(solution)/shard_map/ppermute | solution.py:20
  28.1 37.0 %collective-permute-start.2 = (bf16[128,4096]{1,0:T(8,128)(2,1)S(1)}, bf16[128,4096]{1,0:T(8,128)(2,1)}, u32[]{:S(2)}, u32[]{:S(2)}) collective-permute-start(bf16[128,4096]{1,0:T(8,128)(2,1)S(1)} %get-tuple-element.30.refs_1_), channel_id=1, source_target_pairs={{0,3},{1,0},{2,1},{3,2},{4,7},{5,4},{6,5},{7,6},{8,11},{9,8},{10,9... | collective-permute-start | bytes 3145736 | tf_op jit(solution)/shard_map/ppermute | solution.py:20
  30.7 21.8 %collective-permute-start.4 = (s32[256]{0:T(256)S(1)}, s32[256]{0:T(256)S(1)}, u32[]{:S(2)}, u32[]{:S(2)}) collective-permute-start(s32[256]{0:T(256)S(1)} %bitcast.32), channel_id=1, source_target_pairs={{0,3},{1,0},{2,1},{3,2},{4,7},{5,4},{6,5},{7,6},{8,11},{9,8},{10,9... | collective-permute-start | bytes 3080 | tf_op jit(solution)/shard_map/ppermute | solution.py:20
  30.8 22.9 %collective-permute-start.5 = (s32[256]{0:T(256)S(1)}, s32[256]{0:T(256)S(1)}, u32[]{:S(2)}, u32[]{:S(2)}) collective-permute-start(s32[256]{0:T(256)S(1)} %bitcast.33), channel_id=1, source_target_pairs={{0,1},{1,2},{2,3},{3,0},{4,5},{5,6},{6,7},{7,4},{8,9},{9,10},{10,1... | collective-permute-start | bytes 3080 | tf_op jit(solution)/shard_map/ppermute | solution.py:20
  32.2 21.5 %collective-permute-start.6 = (s32[256]{0:T(256)S(1)}, s32[256]{0:T(256)S(1)}, u32[]{:S(2)}, u32[]{:S(2)}) collective-permute-start(s32[256]{0:T(256)S(1)} %bitcast.34), channel_id=1, source_target_pairs={{0,2},{1,3},{2,0},{3,1},{4,6},{5,7},{6,4},{7,5},{8,10},{9,11},{10,... | collective-permute-start | bytes 3080 | tf_op jit(solution)/shard_map/ppermute | solution.py:20
  57.5 23.5 %collective-permute-start.10 = (bf16[128,4096]{1,0:T(8,128)(2,1)S(1)}, bf16[128,4096]{1,0:T(8,128)(2,1)}, u32[]{:S(2)}, u32[]{:S(2)}) collective-permute-start(bf16[128,4096]{1,0:T(8,128)(2,1)S(1)} %get-tuple-element.29.refs_0_), channel_id=1, source_target_pairs={{0,3},{1,0},{2,1},{3,2},{4,7},{5,4},{6,5},{7,6},{8,11},{9,8},{10,9... | collective-permute-start | bytes 3145736 | tf_op jit(solution)/shard_map/ppermute | solution.py:20
  59.9 24.0 %collective-permute-start.11 = (bf16[128,4096]{1,0:T(8,128)(2,1)S(1)}, bf16[128,4096]{1,0:T(8,128)(2,1)}, u32[]{:S(2)}, u32[]{:S(2)}) collective-permute-start(bf16[128,4096]{1,0:T(8,128)(2,1)S(1)} %get-tuple-element.30.refs_1_), channel_id=1, source_target_pairs={{0,1},{1,2},{2,3},{3,0},{4,5},{5,6},{6,7},{7,4},{8,9},{9,10},{10,1... | collective-permute-start | bytes 3145736 | tf_op jit(solution)/shard_map/ppermute | solution.py:20
  64.9 15.9 %copy-start.7 = (bf16[128,4096]{1,0:T(8,128)(2,1)}, bf16[128,4096]{1,0:T(8,128)(2,1)S(1)}, u32[]{:S(2)}) copy-start(bf16[128,4096]{1,0:T(8,128)(2,1)S(1)} %collective-permute-done.refs_1_) | copy-start | bytes 3145732
  65.0 41.5 %collective-permute-start.1 = (bf16[128,4096]{1,0:T(8,128)(2,1)S(1)}, bf16[128,4096]{1,0:T(8,128)(2,1)}, u32[]{:S(2)}, u32[]{:S(2)}) collective-permute-start(bf16[128,4096]{1,0:T(8,128)(2,1)S(1)} %collective-permute-done.refs_1_), channel_id=1, source_target_pairs={{0,1},{1,2},{2,3},{3,0},{4,5},{5,6},{6,7},{7,4},{8,9},{9,10},{10,1... | collective-permute-start | bytes 3145736 | tf_op jit(solution)/shard_map/ppermute | solution.py:20
  65.0 41.4 %collective-permute-start.3 = (bf16[128,4096]{1,0:T(8,128)(2,1)}, bf16[128,4096]{1,0:T(8,128)(2,1)}, u32[]{:S(2)}, u32[]{:S(2)}) collective-permute-start(bf16[128,4096]{1,0:T(8,128)(2,1)} %collective-permute-done.2.refs_0_), channel_id=1, source_target_pairs={{0,3},{1,0},{2,1},{3,2},{4,7},{5,4},{6,5},{7,6},{8,11},{9,8},{10,9... | collective-permute-start | bytes 3145736 | tf_op jit(solution)/shard_map/ppermute | solution.py:20
  117.9 21.6 %copy-start.9 = (s32[32]{0:T(128)S(1)}, s32[32]{0:T(128)}, u32[]{:S(2)}) copy-start(s32[32]{0:T(128)} %param.10) | copy-start | bytes 388
  117.9 30.2 %all-to-all-start = ((bf16[32,64,256]{2,1,0:T(8,128)(2,1)}), bf16[32,64,256]{2,1,0:T(8,128)(2,1)S(1)}, u32[]{:S(2)}, u32[]{:S(2)}) async-start(bf16[32,64,256]{2,1,0:T(8,128)(2,1)} %get-tuple-element.31), calls=%async_computation | async-start | bytes 2097152 | tf_op jit(solution)/shard_map/all_to_all | solution.py:367
  130.5 28.9 %collective-permute-start.12 = (bf16[256,1024]{1,0:T(8,128)(2,1)}, bf16[256,1024]{1,0:T(8,128)(2,1)S(1)}, u32[]{:S(2)}, u32[]{:S(2)}) collective-permute-start(bf16[256,1024]{1,0:T(8,128)(2,1)} %get-tuple-element.35), channel_id=1, source_target_pairs={{0,2},{1,3},{2,0},{3,1},{4,6},{5,7},{6,4},{7,5},{8,10},{9,11},{10,... | collective-permute-start | bytes 1572872 | tf_op jit(solution)/shard_map/ppermute | solution.py:20
  136.8 22.7 %collective-permute-start.13 = (bf16[256,1024]{1,0:T(8,128)(2,1)}, bf16[256,1024]{1,0:T(8,128)(2,1)S(1)}, u32[]{:S(2)}, u32[]{:S(2)}) collective-permute-start(bf16[256,1024]{1,0:T(8,128)(2,1)} %get-tuple-element.38), channel_id=1, source_target_pairs={{0,1},{1,2},{2,3},{3,0},{4,5},{5,6},{6,7},{7,4},{8,9},{9,10},{10,1... | collective-permute-start | bytes 1572872 | tf_op jit(solution)/shard_map/ppermute | solution.py:20
  136.8 22.7 %collective-permute-start.14 = (bf16[256,1024]{1,0:T(8,128)(2,1)}, bf16[256,1024]{1,0:T(8,128)(2,1)S(1)}, u32[]{:S(2)}, u32[]{:S(2)}) collective-permute-start(bf16[256,1024]{1,0:T(8,128)(2,1)} %get-tuple-element.39), channel_id=1, source_target_pairs={{0,3},{1,0},{2,1},{3,2},{4,7},{5,4},{6,5},{7,6},{8,11},{9,8},{10,9... | collective-permute-start | bytes 1572872 | tf_op jit(solution)/shard_map/ppermute | solution.py:20
  151.5 24.9 %all-to-all-start.1 = ((bf16[32,64,256]{2,1,0:T(8,128)(2,1)}), bf16[32,64,256]{2,1,0:T(8,128)(2,1)S(1)}, u32[]{:S(2)}, u32[]{:S(2)}) async-start(bf16[32,64,256]{2,1,0:T(8,128)(2,1)} %reorder.1), calls=%async_computation.1 | async-start | bytes 2097152 | tf_op jit(solution)/shard_map/all_to_all | solution.py:378
  159.5 1.1 copy-start.6
  (4 other events, 3.7 us)
Sparse Core Ops, SparseCore 0:
  28.1 92.6 all-gather.1
where the time goes:
time: 187 us
  Pallas kernels  66.9 us (36%)
  waiting for transfers between devices  45.8 us (24%)
  starting transfers between devices  37.3 us (20%)
  between operations  19.3 us (10%)
  other arithmetic  11.3 us (6%)
  local copies, waits for them, and re-layouts  5.8 us (3%)
    ppermute x15, waiting for transfers between devices, shifted(): lax.ppermute(value, axis, [(i, (i + by) % count) for i in range(count)])  43.3 us
    pallas_call x3, Pallas kernels, project(): pl.pallas_call(functools.partial(project_kernel, plan), grid=(1,), in_spe...  34.7 us
    ppermute x15, starting transfers between devices, shifted(): lax.ppermute(value, axis, [(i, (i + by) % count) for i in range(count)])  16.7 us
    pallas_call x2, Pallas kernels, attend(): pl.pallas_call(functools.partial(attend_kernel, plan, lots, w_out is not...  14.1 us
    pallas_call x1, Pallas kernels, other_terms(): pl.pallas_call(functools.partial(others_kernel, order), grid=(1,), in_spe...  13.3 us
    all_to_all x1, starting transfers between devices, routed(): scattered = lax.all_to_all(pieces, 'dp', 0, 0, tiled=False)  12.6 us
    all_to_all x1, starting transfers between devices, routed(): return (lax.all_to_all(ordered, 'dp', 0, 0, tiled=False), after)  7.94 us
  transfers between devices with their start and end apart: 18, of which 9 were waited for; matrix products, arithmetic and copies ran while one was open for 6% of the time, Pallas kernels for 35%

commit v1 on v0

v1 whole, which is shorter than its diff:
```python
import functools
import math

import jax
import jax.numpy as jnp
from jax import lax
from jax.experimental import pallas as pl
from jax.experimental.pallas import tpu as pltpu
from jax.sharding import PartitionSpec as P

HD = 128
VMEM_LIMIT = 60 << 20
PROJECT_WEIGHT = 1
LAST_WEIGHT = 120


def shifted(value, axis, by):
    count = lax.axis_size(axis)
    return lax.ppermute(value, axis, [(i, (i + by) % count) for i in range(count)])


def normalised(rows, norm_gain):
    wide = rows.astype(jnp.float32)
    scale = lax.rsqrt(jnp.mean(wide * wide, axis=-1, keepdims=True) + 1e-05)
    return (wide * scale * norm_gain).astype(jnp.bfloat16)


def rotary_tables(positions):
    half = HD // 2
    inverse = 500000.0 ** (-2.0 * jnp.arange(half, dtype=jnp.float32) / HD)
    angles = positions[:, None] * inverse
    cosine, sine = jnp.cos(angles), jnp.sin(angles)
    return (
        jnp.concatenate([cosine, cosine], axis=-1),
        jnp.concatenate([-sine, sine], axis=-1),
    )


def project_kernel(part, plan, *refs):
    rows_ref, held, row_sems, sems = refs[-4:]
    parts = row_sems.shape[0]
    half_refs, refs = refs[:parts], refs[parts:]
    cos_ref, sin_ref, wq_ref, wk_ref, wv_ref = refs[:5]
    refs = refs[5:]
    if part == "all":
        (out_ref,) = refs[:1]
    elif part == "kv":
        own_ref, near_ref, out_ref, pieces_ref = refs[:4]
    else:
        info_ref, first_ref, own_ref, near_ref, far_ref, context_ref, out_ref = refs[:7]
    half = half_refs[0].shape[0]
    count, _, tile = held.shape
    has_kv = part != "q"
    shift = 2 if has_kv else 0

    def source(i):
        if has_kv and i < 2:
            return (wk_ref, wv_ref)[i]
        return wq_ref.at[:, pl.ds((i - shift) * tile, tile)]

    def start(i):
        pltpu.make_async_copy(source(i), held.at[i], sems.at[i]).start()

    moves = [
        pltpu.make_async_copy(ref, rows_ref.at[pl.ds(i * half, half)], row_sems.at[i])
        for i, ref in enumerate(half_refs)
    ]
    for move in moves:
        move.start()
    start(0)
    start(1)
    for move in moves:
        move.wait()

    def one(i, carry):
        pltpu.make_async_copy(wk_ref, held.at[i], sems.at[i]).wait()
        for k in range(2, count):
            pl.when(i == k - 2)(functools.partial(start, k))
        made = jnp.dot(rows_ref[...], held[i], preferred_element_type=jnp.float32)
        cosine, sine = cos_ref[...], sin_ref[...]
        slot = i
        if has_kv:
            cosine = jnp.where(i == 1, 1.0, cosine)
            sine = jnp.where(i == 1, 0.0, sine)
        if part == "all":
            slot = jnp.where(i < 2, i + count - 2, i - 2)
        for at in range(0, tile, HD):
            piece = made[:, at : at + HD]
            piece = piece * cosine + pltpu.roll(piece, HD // 2, 1) * sine
            out_ref[slot, :, at : at + HD] = piece.astype(out_ref.dtype)
        return carry

    lax.fori_loop(0, count, one, 0)
    if part == "all":
        return
    rows = own_ref.shape[1]
    kv_refs = [own_ref, near_ref.at[:, pl.ds(0, rows)], near_ref.at[:, pl.ds(rows, rows)]]
    if part == "kv":
        for kind in (0, 1):
            for slot, kv_ref in enumerate(kv_refs + [out_ref]):
                pieces_ref[kind * 16 : (kind + 1) * 16, slot * 16 : (slot + 1) * 16] = kv_ref[
                    kind
                ].reshape(16, 16, tile)
        return

    def store(head, block):
        context_ref[:, head * HD : (head + 1) * HD] = block

    attend_quarter(
        info_ref, first_ref, kv_refs + [far_ref], {plan[1][0][0]: out_ref}, *plan, store
    )


def whole(shape):
    return pl.BlockSpec(shape, lambda i: (0,) * len(shape))


def kv_block(array):
    last = array.shape[0] // 2 - 1
    return pl.BlockSpec((2,) + array.shape[1:], lambda i: (last, 0, 0))


def project(part, lot, arrived, tables, weights, kv=(), attend_with=None):
    w_query, w_key, w_value = weights
    rows, width = len(arrived) * arrived[0].shape[0], arrived[0].shape[1]
    tile = w_key.shape[1]
    q_tiles = w_query.shape[1] // tile
    count = {"all": q_tiles + 2, "kv": 2, "q": q_tiles}[part]
    anywhere = pl.BlockSpec(memory_space=pl.ANY)
    table = pl.BlockSpec((pl.Element(rows), pl.Element(HD)), lambda i: (lot, 0))
    operands = [*arrived, *tables, w_query, w_key, w_value]
    in_specs = [anywhere] * len(arrived) + [table] * 2 + [anywhere] * 3
    shapes = [(count, rows, tile)]
    scratch, plan = [], None
    if part == "kv":
        shapes.append((32, 64, tile))
    if part == "q":
        info, first_wide, plan = attend_with
        operands += [info, first_wide]
        in_specs += [pl.BlockSpec(memory_space=pltpu.SMEM), whole(first_wide.shape)]
        scratch = [pltpu.VMEM(shapes[0], jnp.bfloat16)]
        shapes = [(rows, q_tiles * tile)]
    operands += kv
    in_specs += [kv_block(array) for array in kv]
    weight = {"all": PROJECT_WEIGHT, "kv": LAST_WEIGHT, "q": 0}[part]
    return pl.pallas_call(
        functools.partial(project_kernel, part, plan),
        grid=(1,),
        in_specs=in_specs,
        out_specs=[whole(shape) for shape in shapes],
        out_shape=[jax.ShapeDtypeStruct(shape, jnp.bfloat16) for shape in shapes],
        scratch_shapes=scratch
        + [
            pltpu.VMEM((rows, width), jnp.bfloat16),
            pltpu.VMEM((count, width, tile), jnp.bfloat16),
            pltpu.SemaphoreType.DMA((len(arrived),)),
            pltpu.SemaphoreType.DMA((count,)),
        ],
        compiler_params=pltpu.CompilerParams(vmem_limit_bytes=VMEM_LIMIT),
        cost_estimate=pl.CostEstimate(
            flops=weight * 2 * rows * width * tile * count,
            bytes_accessed=2 * width * (tile * count + rows),
            transcendentals=0,
        ),
        name="project_" + part,
    )(*operands)


def attend_quarter(info_ref, first_ref, kv_refs, q_refs, slots, q_slots, store):
    blocks, base = info_ref[0], info_ref[1]
    half = first_ref.shape[0] // 8
    rows = 2 * half
    factor = math.log2(math.e) / math.sqrt(HD)
    first = jnp.concatenate(
        [first_ref[lot * rows + at : lot * rows + at + half, :1] for lot, at in q_slots], axis=0
    )

    def run(used):
        count = used * rows
        column = lax.broadcasted_iota(jnp.int32, (rows, count), 1) + (base + rows - count)
        line = lax.broadcasted_iota(jnp.int32, (rows, count), 0) + base
        bias = jnp.where((column >= first) & (column <= line), 0.0, -1e30)
        ones = jnp.ones((count, HD), jnp.bfloat16)
        pieces = slots[2 * (3 - used) :]
        for kv_head in range(2):
            place = slice(kv_head * HD, (kv_head + 1) * HD)
            keys = jnp.concatenate([kv_refs[a][0, at : at + half, place] for a, at in pieces], axis=0)
            values = jnp.concatenate(
                [kv_refs[a][1, at : at + half, place] for a, at in pieces], axis=0
            )
            values = jnp.concatenate([values, ones], axis=1)
            for head in range(4 * kv_head, 4 * kv_head + 4):
                within = slice(head % 2 * HD, (head % 2 + 1) * HD)
                queries = jnp.concatenate(
                    [q_refs[a][head // 2, at : at + half, within] for a, at in q_slots], axis=0
                )
                scores = lax.dot_general(
                    queries, keys, (((1,), (1,)), ((), ())), preferred_element_type=jnp.float32
                )
                scores = scores + bias
                most = jnp.max(scores, axis=-1, keepdims=True)
                weights = jnp.exp2((scores - most) * factor).astype(jnp.bfloat16)
                summed = jnp.dot(weights, values, preferred_element_type=jnp.float32)
                store(head, (summed[:, :HD] / summed[:, HD:]).astype(jnp.bfloat16))

    for used in (1, 2, 3):
        pl.when(blocks == used)(functools.partial(run, used))


def attend_kernel(plan, lots, *refs):
    quarters = len(plan)
    info_refs, first_ref = refs[:quarters], refs[quarters]
    own_ref, near_ref, far_ref = refs[quarters + 1 : quarters + 4]
    rows = own_ref.shape[1]
    kv_refs = [own_ref, near_ref.at[:, pl.ds(0, rows)], near_ref.at[:, pl.ds(rows, rows)], far_ref]
    refs = refs[quarters + 4 :]
    q_refs, out_refs = dict(zip(lots, refs)), refs[len(lots) :]
    for info_ref, out_ref, (slots, q_slots) in zip(info_refs, out_refs, plan):

        def store(head, block, out_ref=out_ref):
            out_ref[:, head * HD : (head + 1) * HD] = block

        attend_quarter(info_ref, first_ref, kv_refs, q_refs, slots, q_slots, store)


def attend_operands(infos, first_wide, kv, queries, plan):
    rows, tile = kv[0].shape[1:]
    tiles = queries[0][0].shape[0] - 2
    lots = [lot for _, _, lot in queries]
    spot = lambda n: pl.BlockSpec((tiles, rows, tile), lambda i: (0, n, 0))
    in_specs = (
        [pl.BlockSpec(memory_space=pltpu.SMEM)] * len(plan)
        + [whole(first_wide.shape)]
        + [kv_block(array) for array in kv]
        + [spot(n) for _, n, _ in queries]
    )
    return lots, in_specs, [*infos, first_wide, *kv, *[array for array, _, _ in queries]]


def attend(infos, first_wide, kv, queries, plan):
    rows, tile = kv[0].shape[1:]
    width = (queries[0][0].shape[0] - 2) * tile
    lots, in_specs, operands = attend_operands(infos, first_wide, kv, queries, plan)
    return pl.pallas_call(
        functools.partial(attend_kernel, plan, lots),
        grid=(1,),
        in_specs=in_specs,
        out_specs=[whole((rows, width))] * len(plan),
        out_shape=[jax.ShapeDtypeStruct((rows, width), jnp.bfloat16)] * len(plan),
        compiler_params=pltpu.CompilerParams(vmem_limit_bytes=VMEM_LIMIT),
        cost_estimate=pl.CostEstimate(flops=0, bytes_accessed=0, transcendentals=0),
        name="attend",
    )(*operands)


def out_kernel(order, *refs):
    stacked, held, sems, context_sems = refs[-4:]
    out_ref = refs[-5]
    w_out_ref, others_ref = refs[-7:-5]
    count = len(order)
    context_refs = refs[: count + 1]
    slots, _, tile = held.shape
    depth = w_out_ref.shape[0]
    steps = out_ref.shape[1] // tile

    def copies(step, slot):
        at = pl.ds(pl.multiple_of(step * tile, tile), tile)
        sources = [w_out_ref.at[:, at]] + [others_ref.at[index, :, at] for index in order]
        return [
            pltpu.make_async_copy(
                source, held.at[slot, pl.ds(i * depth, depth)], sems.at[slot, i]
            )
            for i, source in enumerate(sources)
        ]

    gathers = [
        pltpu.make_async_copy(
            ref, stacked.at[:, pl.ds(i * depth, depth)], context_sems.at[i]
        )
        for i, ref in enumerate(context_refs)
    ]
    for gather in gathers:
        gather.start()
    for step in range(slots - 1):
        for copy in copies(step, step):
            copy.start()
    for gather in gathers:
        gather.wait()

    def one(step, carry):
        slot = lax.rem(step, slots)
        for copy in copies(step, slot):
            copy.wait()

        @pl.when(step + slots - 1 < steps)
        def _():
            for copy in copies(step + slots - 1, lax.rem(step + slots - 1, slots)):
                copy.start()

        total = jnp.dot(stacked[...], held[slot], preferred_element_type=jnp.float32)
        out_ref[:, pl.ds(pl.multiple_of(step * tile, tile), tile)] = total.astype(out_ref.dtype)
        return carry

    lax.fori_loop(0, steps, one, 0)


def out_terms(contexts, order, w_out, others):
    rows, depth = contexts[0].shape
    width = w_out.shape[1]
    tile, slots, count = 512, 4, len(contexts)
    anywhere = pl.BlockSpec(memory_space=pl.ANY)
    return pl.pallas_call(
        functools.partial(out_kernel, order),
        grid=(1,),
        in_specs=[anywhere] * (count + 2),
        out_specs=whole((rows, width)),
        out_shape=jax.ShapeDtypeStruct((rows, width), jnp.bfloat16),
        scratch_shapes=[
            pltpu.VMEM((rows, count * depth), jnp.bfloat16),
            pltpu.VMEM((slots, count * depth, tile), jnp.bfloat16),
            pltpu.SemaphoreType.DMA((slots, count)),
            pltpu.SemaphoreType.DMA((count,)),
        ],
        compiler_params=pltpu.CompilerParams(vmem_limit_bytes=VMEM_LIMIT),
        cost_estimate=pl.CostEstimate(
            flops=2 * count * rows * depth * width,
            bytes_accessed=2 * count * depth * width,
            transcendentals=0,
        ),
        name="out_terms",
    )(*contexts, w_out, others)


def reorder_kernel(source_ref, in_ref, out_ref):
    def one(i, carry):
        out_ref[i] = in_ref[source_ref[i]]
        return carry

    lax.fori_loop(0, in_ref.shape[0], one, 0)


def routed(pieces, source):
    scattered = lax.all_to_all(pieces, "dp", 0, 0, tiled=False)
    ordered = pl.pallas_call(
        reorder_kernel,
        grid=(1,),
        in_specs=[pl.BlockSpec(memory_space=pltpu.SMEM), whole(pieces.shape)],
        out_specs=whole(pieces.shape),
        out_shape=jax.ShapeDtypeStruct(pieces.shape, pieces.dtype),
        name="reorder",
    )(source, scattered)
    return lax.all_to_all(ordered, "dp", 0, 0, tiled=False)


def assemble_kernel(spots, place_ref, pieces_ref, out_ref):
    quarters = len(spots) // 2
    rows = out_ref.shape[0] // quarters
    half = rows // 2
    for quarter in range(quarters):
        base = pl.multiple_of(lax.rem(place_ref[0] + quarter, quarters) * rows, rows)
        for which in (0, 1):
            slot, at = spots[2 * quarter + which]
            for kind in range(2):
                block = pieces_ref[
                    kind * 16 + at // 16 : kind * 16 + (at + half) // 16,
                    slot * 16 : (slot + 1) * 16,
                ].reshape(half, 2 * HD)
                for head in range(2):
                    to = (2 * head + kind) * HD
                    out_ref[pl.ds(base + which * half, half), to : to + HD] = block[
                        :, head * HD : (head + 1) * HD
                    ]


def assemble(spots, place, pieces, shape):
    return pl.pallas_call(
        functools.partial(assemble_kernel, spots),
        grid=(1,),
        in_specs=[pl.BlockSpec(memory_space=pltpu.SMEM), whole(pieces.shape)],
        out_specs=whole(shape),
        out_shape=jax.ShapeDtypeStruct(shape, pieces.dtype),
        name="assemble",
    )(jnp.reshape(place, (1,)).astype(jnp.int32), pieces)


def shards(tokens, doc_ids, destinations, norm_gain, w_query, w_key, w_value, w_out):
    quarters = lax.axis_size("ctx")
    groups = lax.axis_size("dp")
    place = lax.axis_index("ctx")
    row = lax.axis_index("dp")
    rows = tokens.shape[1]
    half = rows // 2

    ids = [doc_ids[0]] + [shifted(doc_ids[0], "ctx", -e) for e in range(1, quarters)]

    share = w_out.shape[0] // groups
    mine = lax.dynamic_slice_in_dim(w_out, row * share, share, 0)
    shares = jnp.stack([shifted(mine, "ctx", e) for e in range(1, quarters)])

    normed = normalised(tokens[0], norm_gain)
    low, high = normed[:half], normed[half:]
    shares, low, high, ids = lax.optimization_barrier((shares, low, high, ids))
    others = lax.all_gather(shares, "dp", axis=1, tiled=True)
    before_low, after_high = shifted(low, "ctx", 1), shifted(high, "ctx", -1)
    halves = [tuple((q, h) for h in (0, 1)) for q in (0, 1, 3, 2)]
    where = {h: (i, j * half) for i, pair in enumerate(halves) for j, h in enumerate(pair)}

    bases = [(place + e) % quarters * rows for e in range(quarters)]
    steps = jnp.arange(half, dtype=jnp.int32)
    order = [h for pair in halves for h in pair]
    row_index = jnp.concatenate([bases[q] + (h * half + steps) for q, h in order])
    row_ids = jnp.concatenate([ids[q][h * half : (h + 1) * half] for q, h in order])
    first = jnp.min(
        jnp.where(row_ids[:, None] == row_ids[None, :], row_index[None, :], quarters * rows), axis=-1
    )
    cosine, sine = rotary_tables((row_index - first).astype(jnp.float32))
    first_wide = jnp.broadcast_to(first[:, None], (first.shape[0], HD))
    infos = []
    for e in range(quarters):
        lot, at = where[(e, 0)]
        least = first[lot * rows + at]
        count = 1 + (least < bases[e]).astype(jnp.int32) + (least < bases[e] - rows).astype(jnp.int32)
        infos.append(jnp.stack([count, bases[e]]))
    anchors = jnp.arange(groups, dtype=jnp.int32)
    source = jnp.sum(jnp.where(destinations[None, :] == anchors[:, None], anchors[None, :], 0), axis=1)
    cosine, sine, first_wide, infos, source = lax.optimization_barrier(
        (cosine, sine, first_wide, infos, source)
    )

    plan = [
        (
            [where[(q % quarters, h)] for q in (e - 2, e - 1, e) for h in (0, 1)],
            [where[(e, h)] for h in (0, 1)],
        )
        for e in range(quarters)
    ]
    weights = (w_query, w_key, w_value)
    tables = (cosine, sine)
    then_low, then_high, _ = lax.optimization_barrier((low, high, first))
    before_high, after_low = shifted(then_high, "ctx", 1), shifted(then_low, "ctx", -1)
    (own,) = project("all", 0, (low, high), tables, weights)
    before_low, after_high, own = lax.optimization_barrier((before_low, after_high, own))
    far = (shifted(before_low, "ctx", 1), shifted(after_high, "ctx", -1))
    arrived = (after_low, after_high, before_low, before_high)
    (near,) = project("all", rows, arrived, tables, weights)
    far_kv, pieces = project("kv", 3 * rows, far, tables, weights, (own, near))
    kv = (own, near, far_kv)
    (opposite,) = project(
        "q", 3 * rows, far, tables, weights, kv, (infos[2], first_wide, plan[2])
    )
    queries = [(near, 0, 1), (near, 1, 2)]
    next_one, previous = attend(
        [infos[1], infos[3]], first_wide, kv, queries, [plan[1], plan[3]]
    )
    received = [shifted(c, "ctx", e) for c, e in ((opposite, 2), (next_one, 1), (previous, 3))]

    delivered = routed(pieces, source)
    (mine_context,) = attend([infos[0]], first_wide, kv, [(own, 0, 0)], [plan[0]])
    attended = out_terms([mine_context, *received], (1, 0, 2), w_out, others)
    delivered, attended = lax.optimization_barrier((delivered, attended))
    spots = tuple(where[(q, h)] for q in range(quarters) for h in (0, 1))
    shape = (quarters * rows, w_key.shape[1] + w_value.shape[1])
    kv_cache = assemble(spots, place, delivered, shape)
    return attended[None], kv_cache[None]


def solution(mesh):
    return jax.shard_map(
        shards,
        mesh=mesh,
        in_specs=(
            P("dp", "ctx", None),
            P("dp", "ctx"),
            P(),
            P(),
            P(None, "ctx"),
            P(None, "ctx"),
            P(None, "ctx"),
            P("ctx", None),
        ),
        out_specs=(P("dp", "ctx", None), P("dp", None, "ctx")),
        check_vma=False,
    )
```

time: 187 us -> 181 us (0.968)
  waiting for transfers between devices: 45.8 us -> 34.3 us
  Pallas kernels: 66.9 us -> 69.3 us
  other arithmetic: 11.3 us -> 13.5 us
    ppermute x15, waiting for transfers between devices: 43.3 us -> 34.3 us  [shifted(): lax.ppermute(value, axis, [(i, (i + by) % count) for i in range(count)])]
    all_to_all x1, starting transfers between devices: 12.6 us -> 10.1 us  [routed(): scattered = lax.all_to_all(pieces, 'dp', 0, 0, tiled=False)]
    all_to_all x1, waiting for transfers between devices: 2.44 us -> 0.01 us  [routed(): return lax.all_to_all(ordered, 'dp', 0, 0, tiled=False)]
    pallas_call x6 -> x7, Pallas kernels: 62.1 us -> 64.4 us  [the longest x4 38.5 us: project(): pl.pallas_call(functools.partial(project_kernel, part, plan), grid=(1,),...]
    unnamed x26 -> x23, local copies, waits for them, and re-layouts: 3.12 us -> 3.8 us
  transfers between devices with their start and end apart: 18 -> 18, of which waited for: 9 -> 6; matrix products, arithmetic and copies ran while one was open for 6% -> 8% of each run, Pallas kernels for 35% -> 37%
where the time goes in v1:
time: 181 us; the launch traced here: 180 us
  Pallas kernels  69.3 us (38%)
  starting transfers between devices  36.9 us (20%)
  waiting for transfers between devices  34.3 us (19%)
  between operations  19.4 us (11%)
  other arithmetic  13.5 us (7%)
  local copies, waits for them, and re-layouts  6.51 us (4%)
    pallas_call x4, Pallas kernels, project(): pl.pallas_call(functools.partial(project_kernel, part, plan), grid=(1,),...  38.5 us
    ppermute x15, waiting for transfers between devices, shifted(): lax.ppermute(value, axis, [(i, (i + by) % count) for i in range(count)])  34.3 us
    ppermute x15, starting transfers between devices, shifted(): lax.ppermute(value, axis, [(i, (i + by) % count) for i in range(count)])  18.1 us
    pallas_call x1, Pallas kernels, out_terms(): pl.pallas_call(functools.partial(out_kernel, order), grid=(1,), in_specs=...  16.5 us
    all_to_all x1, starting transfers between devices, routed(): scattered = lax.all_to_all(pieces, 'dp', 0, 0, tiled=False)  10.1 us
    pallas_call x2, Pallas kernels, attend(): pl.pallas_call(functools.partial(attend_kernel, plan, lots), grid=(1,), i...  9.48 us
    all_to_all x1, starting transfers between devices, routed(): return lax.all_to_all(ordered, 'dp', 0, 0, tiled=False)  8.72 us
    unnamed x23, local copies, waits for them, and re-layouts  3.8 us
  transfers between devices with their start and end apart: 18, of which 6 were waited for; matrix products, arithmetic and copies ran while one was open for 8% of the time, Pallas kernels for 37%

profile of v1, /device:TPU:1, one launch (start us, length us, event | category | flops | bytes accessed | tf_op | source)
XLA Modules:
  0.0 179.8 jit_solution(14304211936116608615)
XLA Ops:
  8.2 3.4 %collective-permute-start.2 = (bf16[32,4096]{1,0:T(8,128)(2,1)S(1)}, bf16[32,4096]{1,0:T(8,128)(2,1)S(1)}, u32[]{:S(2)}, u32[]{:S(2)}) collective-permute-start(bf16[32,4096]{1,0:T(8,128)(2,1)S(1)} %constant_dynamic-slice_fusion), channel_id=1, source_target_pairs={{0,3},{1,0},{2,1},{3,2},{4,7},{5,4},{6,5},{7,6},{8,11},{9,8},{10,9... | collective-permute-start | bytes 786440 | tf_op jit(solution)/shard_map/ppermute | solution.py:19
  12.7 2.1 %collective-permute-start.3 = (s32[256]{0:T(256)}, s32[256]{0:T(256)S(1)}, u32[]{:S(2)}, u32[]{:S(2)}) collective-permute-start(s32[256]{0:T(256)} %bitcast.28), channel_id=1, source_target_pairs={{0,3},{1,0},{2,1},{3,2},{4,7},{5,4},{6,5},{7,6},{8,11},{9,8},{10,9... | collective-permute-start | bytes 3080 | tf_op jit(solution)/shard_map/ppermute | solution.py:19
  16.0 2.1 %fusion = f32[256]{0:T(256)S(1)} fusion(bf16[1,256,4096]{2,1,0:T(8,128)(2,1)} %param.8), kind=kLoop, calls=%fused_computation.2 | loop fusion | flops 3145472 | bytes 2098176 | tf_op jit(solution)/shard_map/reduce_sum | solution.py:24
  18.1 2.2 %fusion.2 = bf16[256,4096]{1,0:T(8,128)(2,1)S(1)} fusion(bf16[1,256,4096]{2,1,0:T(8,128)(2,1)} %param.8, f32[4096]{0:T(1024)} %param.11, f32[256]{0:T(256)S(1)} %add_rsqrt_fusion), kind=kLoop, calls=%fused_computation.4 | loop fusion | flops 4194304 | bytes 4211712 | tf_op jit(solution)/shard_map/convert_element_type | solution.py:25
  20.6 6.3 %collective-permute-done = bf16[32,4096]{1,0:T(8,128)(2,1)S(1)} collective-permute-done((bf16[32,4096]{1,0:T(8,128)(2,1)S(1)}, bf16[32,4096]{1,0:T(8,128)(2,1)S(1)}, u32[]{:S(2)}, u32[]{:S(2)}) %collective-permute-start) | collective-permute-done | bytes 262176 | tf_op jit(solution)/shard_map/ppermute | solution.py:19
  28.8 2.7 %collective-permute-start.7 = (bf16[128,4096]{1,0:T(8,128)(2,1)S(1)}, bf16[128,4096]{1,0:T(8,128)(2,1)}, u32[]{:S(2)}, u32[]{:S(2)}) collective-permute-start(bf16[128,4096]{1,0:T(8,128)(2,1)S(1)} %get-tuple-element.41.refs_1_), channel_id=1, source_target_pairs={{0,3},{1,0},{2,1},{3,2},{4,7},{5,4},{6,5},{7,6},{8,11},{9,8},{10,9... | collective-permute-start | bytes 3145736 | tf_op jit(solution)/shard_map/ppermute | solution.py:19
  35.4 1.5 collective-permute-start.11
  36.9 2.9 %fusion.3 = (f32[1024,64]{1,0:T(8,128)S(1)}, f32[1024,64]{1,0:T(8,128)S(1)}, f32[1024,64]{1,0:T(8,128)}) fusion(f32[64]{0:T(128)S(1)} %multiply_power_fusion, f32[1024]{0:T(1024)S(1)} %subtract_convert_fusion), kind=kLoop, calls=%fused_computation.11 | loop fusion | flops 131072 | bytes 790784 | tf_op jit(solution)/shard_map/neg | solution.py:35
  43.6 2.5 %pad_maximum_fusion.1 = (f32[1024,128]{1,0:T(8,128)}, f32[1024,128]{1,0:T(8,128)}) fusion(f32[1024,64]{1,0:T(8,128)} %get-tuple-element.58, f32[1024,64]{1,0:T(8,128)S(1)} %get-tuple-element.57, f32[1024,64]{1,0:T(8,128)S(1)} %get-tuple-element.56), kind=kLoop, calls=%fused_computation.9 | loop fusion | flops 262144 | bytes 1835008 | tf_op jit(solution)/shard_map/concatenate | solution.py:34
  47.1 9.3 %project_all.2.refs_7_.refs_2_.refs_5_.refs_9_.refs_3_ = bf16[6,256,256]{2,1,0:T(8,128)(2,1)} custom-call(bf16[128,4096]{1,0:T(8,128)(2,1)} %copy-done.3, bf16[128,4096]{1,0:T(8,128)(2,1)} %copy-done.2, f32[1024,128]{1,0:T(8,128)} %get-tuple-element.35.refs_2_.refs_4_, f32[1024,128]{1,0:T(8,128)} %get-tuple-element.36.refs_3_.refs_5_, ...), custom_call_target="tpu_custom_call" | custom-call | flops 3221225472 | bytes 14680064 | tf_op jit(solution)/shard_map/project_all/pallas_call | solution.py:146
  56.6 2.7 %collective-permute-start.9 = (bf16[128,4096]{1,0:T(8,128)(2,1)}, bf16[128,4096]{1,0:T(8,128)(2,1)}, u32[]{:S(2)}, u32[]{:S(2)}) collective-permute-start(bf16[128,4096]{1,0:T(8,128)(2,1)} %collective-permute-done.7.refs_1_), channel_id=1, source_target_pairs={{0,3},{1,0},{2,1},{3,2},{4,7},{5,4},{6,5},{7,6},{8,11},{9,8},{10,9... | collective-permute-start | bytes 3145736 | tf_op jit(solution)/shard_map/ppermute | solution.py:19
  59.2 15.8 %collective-permute-done.10.refs_0_ = bf16[128,4096]{1,0:T(8,128)(2,1)} collective-permute-done((bf16[128,4096]{1,0:T(8,128)(2,1)S(1)}, bf16[128,4096]{1,0:T(8,128)(2,1)}, u32[]{:S(2)}, u32[]{:S(2)}) %collective-permute-start.10) | collective-permute-done | bytes 1048608 | tf_op jit(solution)/shard_map/ppermute | solution.py:19
  76.1 13.5 %project_all.3.refs_8_.refs_3_.refs_10_.refs_4_.refs_6_.refs_7_ = bf16[6,512,256]{2,1,0:T(8,128)(2,1)} custom-call(bf16[128,4096]{1,0:T(8,128)(2,1)} %collective-permute-done.10.refs_0_, bf16[128,4096]{1,0:T(8,128)(2,1)} %collective-permute-done.7.refs_1_, bf16[128,4096]{1,0:T(8,128)(2,1)} %collective-permute-done.6.refs_2_, ...), custom_call_target="tpu_custom_call" | custom-call | flops 6442450944 | bytes 16777216 | tf_op jit(solution)/shard_map/project_all/pallas_call | solution.py:146
  89.6 9.0 %collective-permute-done.8.refs_0_ = bf16[128,4096]{1,0:T(8,128)(2,1)S(1)} collective-permute-done((bf16[128,4096]{1,0:T(8,128)(2,1)}, bf16[128,4096]{1,0:T(8,128)(2,1)S(1)}, u32[]{:S(2)}, u32[]{:S(2)}) %collective-permute-start.8) | collective-permute-done | bytes 1048608 | tf_op jit(solution)/shard_map/ppermute | solution.py:19
  99.6 6.2 %project_kv.1 = (bf16[2,256,256]{2,1,0:T(8,128)(2,1)}, bf16[32,64,256]{2,1,0:T(8,128)(2,1)}) custom-call(bf16[128,4096]{1,0:T(8,128)(2,1)} %copy-done.4, bf16[128,4096]{1,0:T(8,128)(2,1)} %collective-permute-done.9.refs_1_, f32[1024,128]{1,0:T(8,128)} %get-tuple-element.35.refs_2_.refs_4_, f32[1024,128]{1,0:T(8,128)} %get-tuple-element.36.refs_3_.refs_5_, ...), custom_call_target="tpu_custom_call" | custom-call | flops 128849018880 | bytes 6291456 | tf_op jit(solution)/shard_map/project_kv/pallas_call | solution.py:146
  105.8 10.1 %all-to-all-start = ((bf16[32,64,256]{2,1,0:T(8,128)(2,1)}), bf16[32,64,256]{2,1,0:T(8,128)(2,1)S(1)}, u32[]{:S(2)}, u32[]{:S(2)}) async-start(bf16[32,64,256]{2,1,0:T(8,128)(2,1)} %get-tuple-element.42), calls=%async_computation | async-start | bytes 2097152 | tf_op jit(solution)/shard_map/all_to_all | solution.py:343
  115.9 9.4 %project_q.1 = bf16[256,1024]{1,0:T(8,128)(2,1)} custom-call(bf16[128,4096]{1,0:T(8,128)(2,1)} %copy-done.4, bf16[128,4096]{1,0:T(8,128)(2,1)} %collective-permute-done.9.refs_1_, f32[1024,128]{1,0:T(8,128)} %get-tuple-element.35.refs_2_.refs_4_, f32[1024,128]{1,0:T(8,128)} %get-tuple-element.36.refs_3_.refs_5_, bf16[4096,1024]{1,0:T(8,128)(2,1)} %refs_4_.6, ...), custom_call_target="tpu_custom_call" | custom-call | bytes 10485760 | tf_op jit(solution)/shard_map/project_q/pallas_call | solution.py:146
  125.9 6.2 %attend.3 = (bf16[256,1024]{1,0:T(8,128)(2,1)}, bf16[256,1024]{1,0:T(8,128)(2,1)}) custom-call(s32[2]{0:T(128)} %get-tuple-element.47.refs_0_, s32[2]{0:T(128)} %get-tuple-element.48.refs_1_, s32[1024,128]{1,0:T(8,128)} %broadcast_in_dim.48.refs_1_.refs_8_.refs_2_, bf16[6,256,256]{2,1,0:T(8,128)(2,1)} %project_all.2.refs_7_.refs_2_.refs_5_.refs_9_.refs_3_, ...), custom_call_target="tpu_custom_call" | custom-call | tf_op jit(solution)/shard_map/attend/pallas_call | solution.py:244
  135.7 2.5 %reorder.1 = bf16[32,64,256]{2,1,0:T(8,128)(2,1)} custom-call(s32[32]{0:T(128)} %select_reduce_fusion.1.source_ref, bf16[32,64,256]{2,1,0:T(8,128)(2,1)} %copy-done.1), custom_call_target="tpu_custom_call" | custom-call | tf_op jit(solution)/shard_map/reorder/pallas_call | solution.py:344
  138.2 8.7 %all-to-all-start.1 = ((bf16[32,64,256]{2,1,0:T(8,128)(2,1)}), bf16[32,64,256]{2,1,0:T(8,128)(2,1)S(1)}, u32[]{:S(2)}, u32[]{:S(2)}) async-start(bf16[32,64,256]{2,1,0:T(8,128)(2,1)} %reorder.1), calls=%async_computation.1 | async-start | bytes 2097152 | tf_op jit(solution)/shard_map/all_to_all | solution.py:352
  146.9 3.3 %attend.2.refs_0_ = bf16[256,1024]{1,0:T(8,128)(2,1)} custom-call(s32[2]{0:T(128)} %get-tuple-element.43.refs_0_, s32[1024,128]{1,0:T(8,128)} %broadcast_in_dim.48.refs_1_.refs_8_.refs_2_, bf16[6,256,256]{2,1,0:T(8,128)(2,1)} %project_all.2.refs_7_.refs_2_.refs_5_.refs_9_.refs_3_, ...), custom_call_target="tpu_custom_call" | custom-call | tf_op jit(solution)/shard_map/attend/pallas_call | solution.py:244
  150.2 1.9 %collective-permute-done.13.refs_2_ = bf16[256,1024]{1,0:T(8,128)(2,1)S(1)} collective-permute-done((bf16[256,1024]{1,0:T(8,128)(2,1)}, bf16[256,1024]{1,0:T(8,128)(2,1)S(1)}, u32[]{:S(2)}, u32[]{:S(2)}) %collective-permute-start.13) | collective-permute-done | bytes 524320 | tf_op jit(solution)/shard_map/ppermute | solution.py:19
  153.1 16.5 %out_terms.1 = bf16[256,4096]{1,0:T(8,128)(2,1)} custom-call(bf16[256,1024]{1,0:T(8,128)(2,1)} %attend.2.refs_0_, bf16[256,1024]{1,0:T(8,128)(2,1)} %copy-done.5, bf16[256,1024]{1,0:T(8,128)(2,1)} %copy-done.6, bf16[256,1024]{1,0:T(8,128)(2,1)} %copy-done.7, bf16[1024,4096]{1,0:T(8,128)(2,1)} %refs_4_.7, ...), custom_call_target="tpu_custom_call" | custom-call | flops 8589934592 | bytes 33554432 | tf_op jit(solution)/shard_map/out_terms/pallas_call | solution.py:312
  170.7 2.3 %assemble.1 = bf16[1024,512]{1,0:T(8,128)(2,1)} custom-call(s32[1]{0:T(128)} %bitcast.19.place_ref, bf16[32,64,256]{2,1,0:T(8,128)(2,1)} %copy-done), custom_call_target="tpu_custom_call" | custom-call | tf_op jit(solution)/shard_map/assemble/pallas_call | solution.py:376
  (72 shorter events, 17.4 us)
Async XLA Ops:
  7.2 145.1 %all-gather.2.cloned.1.call-start = ((), (), s32[]{:S(2)}) async-start(), calls=%async_computation.2 | async-start | bytes 25952256 | tf_op jit(solution)/shard_map/all_gather | solution.py:403
  8.2 12.3 %collective-permute-start.2 = (bf16[32,4096]{1,0:T(8,128)(2,1)S(1)}, bf16[32,4096]{1,0:T(8,128)(2,1)S(1)}, u32[]{:S(2)}, u32[]{:S(2)}) collective-permute-start(bf16[32,4096]{1,0:T(8,128)(2,1)S(1)} %constant_dynamic-slice_fusion), channel_id=1, source_target_pairs={{0,3},{1,0},{2,1},{3,2},{4,7},{5,4},{6,5},{7,6},{8,11},{9,8},{10,9... | collective-permute-start | bytes 786440 | tf_op jit(solution)/shard_map/ppermute | solution.py:19
  11.6 9.1 %collective-permute-start.1 = (bf16[32,4096]{1,0:T(8,128)(2,1)S(1)}, bf16[32,4096]{1,0:T(8,128)(2,1)S(1)}, u32[]{:S(2)}, u32[]{:S(2)}) collective-permute-start(bf16[32,4096]{1,0:T(8,128)(2,1)S(1)} %constant_dynamic-slice_fusion), channel_id=1, source_target_pairs={{0,2},{1,3},{2,0},{3,1},{4,6},{5,7},{6,4},{7,5},{8,10},{9,11},{10,... | collective-permute-start | bytes 786440 | tf_op jit(solution)/shard_map/ppermute | solution.py:19
  12.1 14.8 %collective-permute-start = (bf16[32,4096]{1,0:T(8,128)(2,1)S(1)}, bf16[32,4096]{1,0:T(8,128)(2,1)S(1)}, u32[]{:S(2)}, u32[]{:S(2)}) collective-permute-start(bf16[32,4096]{1,0:T(8,128)(2,1)S(1)} %constant_dynamic-slice_fusion), channel_id=1, source_target_pairs={{0,1},{1,2},{2,3},{3,0},{4,5},{5,6},{6,7},{7,4},{8,9},{9,10},{10,1... | collective-permute-start | bytes 786440 | tf_op jit(solution)/shard_map/ppermute | solution.py:19
  12.7 15.2 %collective-permute-start.3 = (s32[256]{0:T(256)}, s32[256]{0:T(256)S(1)}, u32[]{:S(2)}, u32[]{:S(2)}) collective-permute-start(s32[256]{0:T(256)} %bitcast.28), channel_id=1, source_target_pairs={{0,3},{1,0},{2,1},{3,2},{4,7},{5,4},{6,5},{7,6},{8,11},{9,8},{10,9... | collective-permute-start | bytes 3080 | tf_op jit(solution)/shard_map/ppermute | solution.py:19
  14.8 13.1 %collective-permute-start.4 = (s32[256]{0:T(256)}, s32[256]{0:T(256)S(1)}, u32[]{:S(2)}, u32[]{:S(2)}) collective-permute-start(s32[256]{0:T(256)} %bitcast.29), channel_id=1, source_target_pairs={{0,2},{1,3},{2,0},{3,1},{4,6},{5,7},{6,4},{7,5},{8,10},{9,11},{10,... | collective-permute-start | bytes 3080 | tf_op jit(solution)/shard_map/ppermute | solution.py:19
  18.1 2.4 %copy-start.8 = (s32[1,256]{1,0:T(1,128)S(1)}, s32[1,256]{1,0:T(1,128)}, u32[]{:S(2)}) copy-start(s32[1,256]{1,0:T(1,128)} %param.9) | copy-start | bytes 3076
  20.3 7.8 %copy-start.9 = (s32[32]{0:T(128)S(1)}, s32[32]{0:T(128)}, u32[]{:S(2)}) copy-start(s32[32]{0:T(128)} %param.10) | copy-start | bytes 388
  20.5 26.6 %copy-start.2 = (bf16[128,4096]{1,0:T(8,128)(2,1)}, bf16[128,4096]{1,0:T(8,128)(2,1)S(1)}, u32[]{:S(2)}) copy-start(bf16[128,4096]{1,0:T(8,128)(2,1)S(1)} %get-tuple-element.41.refs_1_) | copy-start | bytes 3145732
  20.5 26.6 %copy-start.3 = (bf16[128,4096]{1,0:T(8,128)(2,1)}, bf16[128,4096]{1,0:T(8,128)(2,1)S(1)}, u32[]{:S(2)}) copy-start(bf16[128,4096]{1,0:T(8,128)(2,1)S(1)} %get-tuple-element.40.refs_0_) | copy-start | bytes 3145732
  20.5 7.3 %collective-permute-start.5 = (s32[256]{0:T(256)S(1)}, s32[256]{0:T(256)S(1)}, u32[]{:S(2)}, u32[]{:S(2)}) collective-permute-start(s32[256]{0:T(256)S(1)} %bitcast.30), channel_id=1, source_target_pairs={{0,1},{1,2},{2,3},{3,0},{4,5},{5,6},{6,7},{7,4},{8,9},{9,10},{10,1... | collective-permute-start | bytes 3080 | tf_op jit(solution)/shard_map/ppermute | solution.py:19
  28.8 27.7 %collective-permute-start.6 = (bf16[128,4096]{1,0:T(8,128)(2,1)S(1)}, bf16[128,4096]{1,0:T(8,128)(2,1)}, u32[]{:S(2)}, u32[]{:S(2)}) collective-permute-start(bf16[128,4096]{1,0:T(8,128)(2,1)S(1)} %get-tuple-element.40.refs_0_), channel_id=1, source_target_pairs={{0,1},{1,2},{2,3},{3,0},{4,5},{5,6},{6,7},{7,4},{8,9},{9,10},{10,1... | collective-permute-start | bytes 3145736 | tf_op jit(solution)/shard_map/ppermute | solution.py:19
  28.8 27.7 %collective-permute-start.7 = (bf16[128,4096]{1,0:T(8,128)(2,1)S(1)}, bf16[128,4096]{1,0:T(8,128)(2,1)}, u32[]{:S(2)}, u32[]{:S(2)}) collective-permute-start(bf16[128,4096]{1,0:T(8,128)(2,1)S(1)} %get-tuple-element.41.refs_1_), channel_id=1, source_target_pairs={{0,3},{1,0},{2,1},{3,2},{4,7},{5,4},{6,5},{7,6},{8,11},{9,8},{10,9... | collective-permute-start | bytes 3145736 | tf_op jit(solution)/shard_map/ppermute | solution.py:19
  35.3 39.7 %collective-permute-start.10 = (bf16[128,4096]{1,0:T(8,128)(2,1)S(1)}, bf16[128,4096]{1,0:T(8,128)(2,1)}, u32[]{:S(2)}, u32[]{:S(2)}) collective-permute-start(bf16[128,4096]{1,0:T(8,128)(2,1)S(1)} %get-tuple-element.40.refs_0_), channel_id=1, source_target_pairs={{0,3},{1,0},{2,1},{3,2},{4,7},{5,4},{6,5},{7,6},{8,11},{9,8},{10,9... | collective-permute-start | bytes 3145736 | tf_op jit(solution)/shard_map/ppermute | solution.py:19
  35.4 40.7 %collective-permute-start.11 = (bf16[128,4096]{1,0:T(8,128)(2,1)S(1)}, bf16[128,4096]{1,0:T(8,128)(2,1)}, u32[]{:S(2)}, u32[]{:S(2)}) collective-permute-start(bf16[128,4096]{1,0:T(8,128)(2,1)S(1)} %get-tuple-element.41.refs_1_), channel_id=1, source_target_pairs={{0,1},{1,2},{2,3},{3,0},{4,5},{5,6},{6,7},{7,4},{8,9},{9,10},{10,1... | collective-permute-start | bytes 3145736 | tf_op jit(solution)/shard_map/ppermute | solution.py:19
  56.5 42.1 %collective-permute-start.8 = (bf16[128,4096]{1,0:T(8,128)(2,1)}, bf16[128,4096]{1,0:T(8,128)(2,1)S(1)}, u32[]{:S(2)}, u32[]{:S(2)}) collective-permute-start(bf16[128,4096]{1,0:T(8,128)(2,1)} %collective-permute-done.6.refs_2_), channel_id=1, source_target_pairs={{0,1},{1,2},{2,3},{3,0},{4,5},{5,6},{6,7},{7,4},{8,9},{9,10},{10,1... | collective-permute-start | bytes 3145736 | tf_op jit(solution)/shard_map/ppermute | solution.py:19
  56.6 42.0 %collective-permute-start.9 = (bf16[128,4096]{1,0:T(8,128)(2,1)}, bf16[128,4096]{1,0:T(8,128)(2,1)}, u32[]{:S(2)}, u32[]{:S(2)}) collective-permute-start(bf16[128,4096]{1,0:T(8,128)(2,1)} %collective-permute-done.7.refs_1_), channel_id=1, source_target_pairs={{0,3},{1,0},{2,1},{3,2},{4,7},{5,4},{6,5},{7,6},{8,11},{9,8},{10,9... | collective-permute-start | bytes 3145736 | tf_op jit(solution)/shard_map/ppermute | solution.py:19
  105.8 28.9 %all-to-all-start = ((bf16[32,64,256]{2,1,0:T(8,128)(2,1)}), bf16[32,64,256]{2,1,0:T(8,128)(2,1)S(1)}, u32[]{:S(2)}, u32[]{:S(2)}) async-start(bf16[32,64,256]{2,1,0:T(8,128)(2,1)} %get-tuple-element.42), calls=%async_computation | async-start | bytes 2097152 | tf_op jit(solution)/shard_map/all_to_all | solution.py:343
  125.3 24.9 %collective-permute-start.12 = (bf16[256,1024]{1,0:T(8,128)(2,1)}, bf16[256,1024]{1,0:T(8,128)(2,1)S(1)}, u32[]{:S(2)}, u32[]{:S(2)}) collective-permute-start(bf16[256,1024]{1,0:T(8,128)(2,1)} %project_q.1), channel_id=1, source_target_pairs={{0,2},{1,3},{2,0},{3,1},{4,6},{5,7},{6,4},{7,5},{8,10},{9,11},{10,... | collective-permute-start | bytes 1572872 | tf_op jit(solution)/shard_map/ppermute | solution.py:19
  132.0 20.1 %collective-permute-start.13 = (bf16[256,1024]{1,0:T(8,128)(2,1)}, bf16[256,1024]{1,0:T(8,128)(2,1)S(1)}, u32[]{:S(2)}, u32[]{:S(2)}) collective-permute-start(bf16[256,1024]{1,0:T(8,128)(2,1)} %get-tuple-element.49), channel_id=1, source_target_pairs={{0,1},{1,2},{2,3},{3,0},{4,5},{5,6},{6,7},{7,4},{8,9},{9,10},{10,1... | collective-permute-start | bytes 1572872 | tf_op jit(solution)/shard_map/ppermute | solution.py:19
  133.4 18.9 %collective-permute-start.14 = (bf16[256,1024]{1,0:T(8,128)(2,1)}, bf16[256,1024]{1,0:T(8,128)(2,1)S(1)}, u32[]{:S(2)}, u32[]{:S(2)}) collective-permute-start(bf16[256,1024]{1,0:T(8,128)(2,1)} %get-tuple-element.50), channel_id=1, source_target_pairs={{0,3},{1,0},{2,1},{3,2},{4,7},{5,4},{6,5},{7,6},{8,11},{9,8},{10,9... | collective-permute-start | bytes 1572872 | tf_op jit(solution)/shard_map/ppermute | solution.py:19
  138.2 31.5 %all-to-all-start.1 = ((bf16[32,64,256]{2,1,0:T(8,128)(2,1)}), bf16[32,64,256]{2,1,0:T(8,128)(2,1)S(1)}, u32[]{:S(2)}, u32[]{:S(2)}) async-start(bf16[32,64,256]{2,1,0:T(8,128)(2,1)} %reorder.1), calls=%async_computation.1 | async-start | bytes 2097152 | tf_op jit(solution)/shard_map/all_to_all | solution.py:352
  150.2 2.1 %copy-start.5 = (bf16[256,1024]{1,0:T(8,128)(2,1)}, bf16[256,1024]{1,0:T(8,128)(2,1)S(1)}, u32[]{:S(2)}) copy-start(bf16[256,1024]{1,0:T(8,128)(2,1)S(1)} %collective-permute-done.12.refs_1_) | copy-start | bytes 1572868
  169.7 1.0 copy-start
  (4 other events, 3.6 us)
Sparse Core Ops, SparseCore 0:
  28.0 94.4 all-gather.1

commit v2 on v1

--- a/solution.py
+++ b/solution.py
@@ -307,7 +307,7 @@
 def out_terms(contexts, order, w_out, others):
     rows, depth = contexts[0].shape
     width = w_out.shape[1]
-    tile, slots, count = 512, 4, len(contexts)
+    tile, slots, count = 512, 3, len(contexts)
     anywhere = pl.BlockSpec(memory_space=pl.ANY)
     return pl.pallas_call(
         functools.partial(out_kernel, order),
@@ -379,6 +379,7 @@
         in_specs=[pl.BlockSpec(memory_space=pltpu.SMEM), whole(pieces.shape)],
         out_specs=whole(shape),
         out_shape=jax.ShapeDtypeStruct(shape, pieces.dtype),
+        compiler_params=pltpu.CompilerParams(vmem_limit_bytes=16 << 20),
         name="assemble",
     )(jnp.reshape(place, (1,)).astype(jnp.int32), pieces)
 
@@ -443,15 +444,14 @@
     far = (shifted(before_low, "ctx", 1), shifted(after_high, "ctx", -1))
     arrived = (after_low, after_high, before_low, before_high)
     (near,) = project("all", rows, arrived, tables, weights)
+    (next_one,) = attend([infos[1]], first_wide, (own, near, own), [(near, 0, 1)], [plan[1]])
+    *far, next_one = lax.optimization_barrier((*far, next_one))
     far_kv, pieces = project("kv", 3 * rows, far, tables, weights, (own, near))
     kv = (own, near, far_kv)
     (opposite,) = project(
         "q", 3 * rows, far, tables, weights, kv, (infos[2], first_wide, plan[2])
     )
-    queries = [(near, 0, 1), (near, 1, 2)]
-    next_one, previous = attend(
-        [infos[1], infos[3]], first_wide, kv, queries, [plan[1], plan[3]]
-    )
+    (previous,) = attend([infos[3]], first_wide, kv, [(near, 1, 2)], [plan[3]])
     received = [shifted(c, "ctx", e) for c, e in ((opposite, 2), (next_one, 1), (previous, 3))]
 
     delivered = routed(pieces, source)

time: 181 us -> 177 us (0.978)
  waiting for transfers between devices: 34.3 us -> 31.3 us
    ppermute x15, waiting for transfers between devices: 34.3 us -> 31.1 us  [shifted(): lax.ppermute(value, axis, [(i, (i + by) % count) for i in range(count)])]
    pallas_call x2 -> x3, Pallas kernels: 9.48 us -> 11.7 us  [attend(): pl.pallas_call(functools.partial(attend_kernel, plan, lots), grid=(1,), i...]
  transfers between devices with their start and end apart: 18 -> 18, of which waited for: 6 -> 7; matrix products, arithmetic and copies ran while one was open for 8% -> 9% of each run, Pallas kernels for 37% -> 38%
where the time goes in v2:
time: 177 us; the launch traced here: 176 us
  Pallas kernels  68.9 us (39%)
  starting transfers between devices  37.5 us (21%)
  waiting for transfers between devices  31.3 us (18%)
  between operations  19.4 us (11%)
  other arithmetic  13.5 us (8%)
  local copies, waits for them, and re-layouts  5.59 us (3%)
    pallas_call x4, Pallas kernels, project(): pl.pallas_call(functools.partial(project_kernel, part, plan), grid=(1,),...  38.3 us
    ppermute x15, waiting for transfers between devices, shifted(): lax.ppermute(value, axis, [(i, (i + by) % count) for i in range(count)])  31.1 us
    ppermute x15, starting transfers between devices, shifted(): lax.ppermute(value, axis, [(i, (i + by) % count) for i in range(count)])  18.1 us
    pallas_call x1, Pallas kernels, out_terms(): pl.pallas_call(functools.partial(out_kernel, order), grid=(1,), in_specs=...  15.3 us
    pallas_call x3, Pallas kernels, attend(): pl.pallas_call(functools.partial(attend_kernel, plan, lots), grid=(1,), i...  11.7 us
    all_to_all x1, starting transfers between devices, routed(): scattered = lax.all_to_all(pieces, 'dp', 0, 0, tiled=False)  10 us
    all_to_all x1, starting transfers between devices, routed(): return lax.all_to_all(ordered, 'dp', 0, 0, tiled=False)  9.35 us
  transfers between devices with their start and end apart: 18, of which 7 were waited for; matrix products, arithmetic and copies ran while one was open for 9% of the time, Pallas kernels for 38%

profile of v2, /device:TPU:1, one launch (start us, length us, event | category | flops | bytes accessed | tf_op | source)
XLA Modules:
  0.0 176.3 jit_solution(2623357653615001151)
XLA Ops:
  8.2 3.4 %collective-permute-start.2 = (bf16[32,4096]{1,0:T(8,128)(2,1)S(1)}, bf16[32,4096]{1,0:T(8,128)(2,1)S(1)}, u32[]{:S(2)}, u32[]{:S(2)}) collective-permute-start(bf16[32,4096]{1,0:T(8,128)(2,1)S(1)} %constant_dynamic-slice_fusion), channel_id=1, source_target_pairs={{0,3},{1,0},{2,1},{3,2},{4,7},{5,4},{6,5},{7,6},{8,11},{9,8},{10,9... | collective-permute-start | bytes 786440 | tf_op jit(solution)/shard_map/ppermute | solution.py:19
  12.7 2.1 %collective-permute-start.3 = (s32[256]{0:T(256)}, s32[256]{0:T(256)S(1)}, u32[]{:S(2)}, u32[]{:S(2)}) collective-permute-start(s32[256]{0:T(256)} %bitcast.28), channel_id=1, source_target_pairs={{0,3},{1,0},{2,1},{3,2},{4,7},{5,4},{6,5},{7,6},{8,11},{9,8},{10,9... | collective-permute-start | bytes 3080 | tf_op jit(solution)/shard_map/ppermute | solution.py:19
  16.0 2.1 %fusion = f32[256]{0:T(256)S(1)} fusion(bf16[1,256,4096]{2,1,0:T(8,128)(2,1)} %param.8), kind=kLoop, calls=%fused_computation.2 | loop fusion | flops 3145472 | bytes 2098176 | tf_op jit(solution)/shard_map/reduce_sum | solution.py:24
  18.1 2.2 %fusion.2 = bf16[256,4096]{1,0:T(8,128)(2,1)S(1)} fusion(bf16[1,256,4096]{2,1,0:T(8,128)(2,1)} %param.8, f32[4096]{0:T(1024)} %param.11, f32[256]{0:T(256)S(1)} %add_rsqrt_fusion), kind=kLoop, calls=%fused_computation.4 | loop fusion | flops 4194304 | bytes 4211712 | tf_op jit(solution)/shard_map/convert_element_type | solution.py:25
  20.6 6.3 %collective-permute-done = bf16[32,4096]{1,0:T(8,128)(2,1)S(1)} collective-permute-done((bf16[32,4096]{1,0:T(8,128)(2,1)S(1)}, bf16[32,4096]{1,0:T(8,128)(2,1)S(1)}, u32[]{:S(2)}, u32[]{:S(2)}) %collective-permute-start) | collective-permute-done | bytes 262176 | tf_op jit(solution)/shard_map/ppermute | solution.py:19
  28.9 2.7 %collective-permute-start.7 = (bf16[128,4096]{1,0:T(8,128)(2,1)S(1)}, bf16[128,4096]{1,0:T(8,128)(2,1)}, u32[]{:S(2)}, u32[]{:S(2)}) collective-permute-start(bf16[128,4096]{1,0:T(8,128)(2,1)S(1)} %get-tuple-element.44.refs_1_), channel_id=1, source_target_pairs={{0,3},{1,0},{2,1},{3,2},{4,7},{5,4},{6,5},{7,6},{8,11},{9,8},{10,9... | collective-permute-start | bytes 3145736 | tf_op jit(solution)/shard_map/ppermute | solution.py:19
  37.0 3.0 %fusion.3 = (f32[1024,64]{1,0:T(8,128)S(1)}, f32[1024,64]{1,0:T(8,128)S(1)}, f32[1024,64]{1,0:T(8,128)}) fusion(f32[64]{0:T(128)S(1)} %multiply_power_fusion, f32[1024]{0:T(1024)S(1)} %subtract_convert_fusion), kind=kLoop, calls=%fused_computation.11 | loop fusion | flops 131072 | bytes 790784 | tf_op jit(solution)/shard_map/neg | solution.py:35
  43.6 2.6 %pad_maximum_fusion.1 = (f32[1024,128]{1,0:T(8,128)}, f32[1024,128]{1,0:T(8,128)}) fusion(f32[1024,64]{1,0:T(8,128)} %get-tuple-element.60, f32[1024,64]{1,0:T(8,128)S(1)} %get-tuple-element.59, f32[1024,64]{1,0:T(8,128)S(1)} %get-tuple-element.58), kind=kLoop, calls=%fused_computation.9 | loop fusion | flops 262144 | bytes 1835008 | tf_op jit(solution)/shard_map/concatenate | solution.py:34
  47.2 9.4 %project_all.2.refs_2_.refs_4_.refs_7_.refs_5_.refs_9_ = bf16[6,256,256]{2,1,0:T(8,128)(2,1)} custom-call(bf16[128,4096]{1,0:T(8,128)(2,1)} %copy-done.2, bf16[128,4096]{1,0:T(8,128)(2,1)} %copy-done.1, f32[1024,128]{1,0:T(8,128)} %get-tuple-element.36.refs_2_.refs_4_, f32[1024,128]{1,0:T(8,128)} %get-tuple-element.37.refs_3_.refs_5_, ...), custom_call_target="tpu_custom_call" | custom-call | flops 3221225472 | bytes 14680064 | tf_op jit(solution)/shard_map/project_all/pallas_call | solution.py:146
  56.7 2.6 %collective-permute-start.9 = (bf16[128,4096]{1,0:T(8,128)(2,1)}, bf16[128,4096]{1,0:T(8,128)(2,1)}, u32[]{:S(2)}, u32[]{:S(2)}) collective-permute-start(bf16[128,4096]{1,0:T(8,128)(2,1)} %collective-permute-done.7.refs_1_), channel_id=1, source_target_pairs={{0,3},{1,0},{2,1},{3,2},{4,7},{5,4},{6,5},{7,6},{8,11},{9,8},{10,9... | collective-permute-start | bytes 3145736 | tf_op jit(solution)/shard_map/ppermute | solution.py:19
  59.3 15.7 %collective-permute-done.10.refs_0_ = bf16[128,4096]{1,0:T(8,128)(2,1)} collective-permute-done((bf16[128,4096]{1,0:T(8,128)(2,1)S(1)}, bf16[128,4096]{1,0:T(8,128)(2,1)}, u32[]{:S(2)}, u32[]{:S(2)}) %collective-permute-start.10) | collective-permute-done | bytes 1048608 | tf_op jit(solution)/shard_map/ppermute | solution.py:19
  76.2 13.5 %project_all.3.refs_3_.refs_5_.refs_8_.refs_10_ = bf16[6,512,256]{2,1,0:T(8,128)(2,1)} custom-call(bf16[128,4096]{1,0:T(8,128)(2,1)} %collective-permute-done.10.refs_0_, bf16[128,4096]{1,0:T(8,128)(2,1)} %collective-permute-done.7.refs_1_, bf16[128,4096]{1,0:T(8,128)(2,1)} %collective-permute-done.6.refs_2_, ...), custom_call_target="tpu_custom_call" | custom-call | flops 6442450944 | bytes 16777216 | tf_op jit(solution)/shard_map/project_all/pallas_call | solution.py:146
  89.7 4.2 %attend.3 = bf16[256,1024]{1,0:T(8,128)(2,1)} custom-call(s32[2]{0:T(128)} %get-tuple-element.40.refs_0_, s32[1024,128]{1,0:T(8,128)} %broadcast_in_dim.48.refs_1_.refs_8_, bf16[6,256,256]{2,1,0:T(8,128)(2,1)} %project_all.2.refs_2_.refs_4_.refs_7_.refs_5_.refs_9_, bf16[6,512,256]{2,1,0:T(8,128)(2,1)} %project_all.3.refs_3_.refs_5_.refs_8_.refs_10_, ...), custom_call_target="tpu_custom_call" | custom-call | tf_op jit(solution)/shard_map/attend/pallas_call | solution.py:244
  93.9 4.8 %collective-permute-done.8.refs_0_ = bf16[128,4096]{1,0:T(8,128)(2,1)S(1)} collective-permute-done((bf16[128,4096]{1,0:T(8,128)(2,1)}, bf16[128,4096]{1,0:T(8,128)(2,1)S(1)}, u32[]{:S(2)}, u32[]{:S(2)}) %collective-permute-start.8) | collective-permute-done | bytes 1048608 | tf_op jit(solution)/shard_map/ppermute | solution.py:19
  99.6 6.2 %project_kv.1 = (bf16[2,256,256]{2,1,0:T(8,128)(2,1)}, bf16[32,64,256]{2,1,0:T(8,128)(2,1)}) custom-call(bf16[128,4096]{1,0:T(8,128)(2,1)} %copy-done.3, bf16[128,4096]{1,0:T(8,128)(2,1)} %collective-permute-done.9.refs_1_, f32[1024,128]{1,0:T(8,128)} %get-tuple-element.36.refs_2_.refs_4_, f32[1024,128]{1,0:T(8,128)} %get-tuple-element.37.refs_3_.refs_5_, ...), custom_call_target="tpu_custom_call" | custom-call | flops 128849018880 | bytes 6291456 | tf_op jit(solution)/shard_map/project_kv/pallas_call | solution.py:146
  105.9 10.0 %all-to-all-start = ((bf16[32,64,256]{2,1,0:T(8,128)(2,1)}), bf16[32,64,256]{2,1,0:T(8,128)(2,1)S(1)}, u32[]{:S(2)}, u32[]{:S(2)}) async-start(bf16[32,64,256]{2,1,0:T(8,128)(2,1)} %get-tuple-element.47), calls=%async_computation | async-start | bytes 2097152 | tf_op jit(solution)/shard_map/all_to_all | solution.py:343
  115.9 9.2 %project_q.1 = bf16[256,1024]{1,0:T(8,128)(2,1)} custom-call(bf16[128,4096]{1,0:T(8,128)(2,1)} %copy-done.3, bf16[128,4096]{1,0:T(8,128)(2,1)} %collective-permute-done.9.refs_1_, f32[1024,128]{1,0:T(8,128)} %get-tuple-element.36.refs_2_.refs_4_, f32[1024,128]{1,0:T(8,128)} %get-tuple-element.37.refs_3_.refs_5_, bf16[4096,1024]{1,0:T(8,128)(2,1)} %refs_4_.6, ...), custom_call_target="tpu_custom_call" | custom-call | bytes 10485760 | tf_op jit(solution)/shard_map/project_q/pallas_call | solution.py:146
  125.9 2.6 %collective-permute-start.13 = (bf16[256,1024]{1,0:T(8,128)(2,1)S(1)}, bf16[256,1024]{1,0:T(8,128)(2,1)S(1)}, u32[]{:S(2)}, u32[]{:S(2)}) collective-permute-start(bf16[256,1024]{1,0:T(8,128)(2,1)S(1)} %copy-done.7), channel_id=1, source_target_pairs={{0,1},{1,2},{2,3},{3,0},{4,5},{5,6},{6,7},{7,4},{8,9},{9,10},{10,1... | collective-permute-start | bytes 1572872 | tf_op jit(solution)/shard_map/ppermute | solution.py:19
  128.5 4.2 %attend.5 = bf16[256,1024]{1,0:T(8,128)(2,1)} custom-call(s32[2]{0:T(128)} %get-tuple-element.52.refs_0_, s32[1024,128]{1,0:T(8,128)} %broadcast_in_dim.48.refs_1_.refs_8_, bf16[6,256,256]{2,1,0:T(8,128)(2,1)} %project_all.2.refs_2_.refs_4_.refs_7_.refs_5_.refs_9_, bf16[6,512,256]{2,1,0:T(8,128)(2,1)} %project_all.3.refs_3_.refs_5_.refs_8_.refs_10_, ...), custom_call_target="tpu_custom_call" | custom-call | tf_op jit(solution)/shard_map/attend/pallas_call | solution.py:244
  133.8 2.5 %reorder.1 = bf16[32,64,256]{2,1,0:T(8,128)(2,1)} custom-call(s32[32]{0:T(128)} %select_reduce_fusion.1.source_ref, bf16[32,64,256]{2,1,0:T(8,128)(2,1)} %copy-done), custom_call_target="tpu_custom_call" | custom-call | tf_op jit(solution)/shard_map/reorder/pallas_call | solution.py:344
  136.3 9.3 %all-to-all-start.1 = ((bf16[32,64,256]{2,1,0:T(8,128)(2,1)}), bf16[32,64,256]{2,1,0:T(8,128)(2,1)S(1)}, u32[]{:S(2)}, u32[]{:S(2)}) async-start(bf16[32,64,256]{2,1,0:T(8,128)(2,1)} %reorder.1), calls=%async_computation.1 | async-start | bytes 2097152 | tf_op jit(solution)/shard_map/all_to_all | solution.py:352
  145.6 3.3 %attend.4.refs_0_ = bf16[256,1024]{1,0:T(8,128)(2,1)} custom-call(s32[2]{0:T(128)} %get-tuple-element.48.refs_0_, s32[1024,128]{1,0:T(8,128)} %broadcast_in_dim.48.refs_1_.refs_8_, bf16[6,256,256]{2,1,0:T(8,128)(2,1)} %project_all.2.refs_2_.refs_4_.refs_7_.refs_5_.refs_9_, bf16[6,512,256]{2,1,0:T(8,128)(2,1)} %project_all.3.refs_3_.refs_5_.refs_8_.refs_10_, ...), custom_call_target="tpu_custom_call" | custom-call | tf_op jit(solution)/shard_map/attend/pallas_call | solution.py:244
  149.0 3.1 %collective-permute-done.13.refs_2_ = bf16[256,1024]{1,0:T(8,128)(2,1)S(1)} collective-permute-done((bf16[256,1024]{1,0:T(8,128)(2,1)S(1)}, bf16[256,1024]{1,0:T(8,128)(2,1)S(1)}, u32[]{:S(2)}, u32[]{:S(2)}) %collective-permute-start.13) | collective-permute-done | bytes 524320 | tf_op jit(solution)/shard_map/ppermute | solution.py:19
  153.0 15.3 %out_terms.1 = bf16[256,4096]{1,0:T(8,128)(2,1)} custom-call(bf16[256,1024]{1,0:T(8,128)(2,1)} %attend.4.refs_0_, bf16[256,1024]{1,0:T(8,128)(2,1)} %copy-done.4, bf16[256,1024]{1,0:T(8,128)(2,1)} %copy-done.5, bf16[256,1024]{1,0:T(8,128)(2,1)} %copy-done.6, bf16[1024,4096]{1,0:T(8,128)(2,1)} %refs_4_.7, ...), custom_call_target="tpu_custom_call" | custom-call | flops 8589934592 | bytes 33554432 | tf_op jit(solution)/shard_map/out_terms/pallas_call | solution.py:312
  (73 shorter events, 16.6 us)
Async XLA Ops:
  7.2 145.0 %all-gather.2.cloned.1.call-start = ((), (), s32[]{:S(2)}) async-start(), calls=%async_computation.2 | async-start | bytes 25952256 | tf_op jit(solution)/shard_map/all_gather | solution.py:404
  8.2 12.3 %collective-permute-start.2 = (bf16[32,4096]{1,0:T(8,128)(2,1)S(1)}, bf16[32,4096]{1,0:T(8,128)(2,1)S(1)}, u32[]{:S(2)}, u32[]{:S(2)}) collective-permute-start(bf16[32,4096]{1,0:T(8,128)(2,1)S(1)} %constant_dynamic-slice_fusion), channel_id=1, source_target_pairs={{0,3},{1,0},{2,1},{3,2},{4,7},{5,4},{6,5},{7,6},{8,11},{9,8},{10,9... | collective-permute-start | bytes 786440 | tf_op jit(solution)/shard_map/ppermute | solution.py:19
  11.6 9.1 %collective-permute-start.1 = (bf16[32,4096]{1,0:T(8,128)(2,1)S(1)}, bf16[32,4096]{1,0:T(8,128)(2,1)S(1)}, u32[]{:S(2)}, u32[]{:S(2)}) collective-permute-start(bf16[32,4096]{1,0:T(8,128)(2,1)S(1)} %constant_dynamic-slice_fusion), channel_id=1, source_target_pairs={{0,2},{1,3},{2,0},{3,1},{4,6},{5,7},{6,4},{7,5},{8,10},{9,11},{10,... | collective-permute-start | bytes 786440 | tf_op jit(solution)/shard_map/ppermute | solution.py:19
  12.1 14.8 %collective-permute-start = (bf16[32,4096]{1,0:T(8,128)(2,1)S(1)}, bf16[32,4096]{1,0:T(8,128)(2,1)S(1)}, u32[]{:S(2)}, u32[]{:S(2)}) collective-permute-start(bf16[32,4096]{1,0:T(8,128)(2,1)S(1)} %constant_dynamic-slice_fusion), channel_id=1, source_target_pairs={{0,1},{1,2},{2,3},{3,0},{4,5},{5,6},{6,7},{7,4},{8,9},{9,10},{10,1... | collective-permute-start | bytes 786440 | tf_op jit(solution)/shard_map/ppermute | solution.py:19
  12.7 15.2 %collective-permute-start.3 = (s32[256]{0:T(256)}, s32[256]{0:T(256)S(1)}, u32[]{:S(2)}, u32[]{:S(2)}) collective-permute-start(s32[256]{0:T(256)} %bitcast.28), channel_id=1, source_target_pairs={{0,3},{1,0},{2,1},{3,2},{4,7},{5,4},{6,5},{7,6},{8,11},{9,8},{10,9... | collective-permute-start | bytes 3080 | tf_op jit(solution)/shard_map/ppermute | solution.py:19
  14.8 13.1 %collective-permute-start.4 = (s32[256]{0:T(256)}, s32[256]{0:T(256)S(1)}, u32[]{:S(2)}, u32[]{:S(2)}) collective-permute-start(s32[256]{0:T(256)} %bitcast.29), channel_id=1, source_target_pairs={{0,2},{1,3},{2,0},{3,1},{4,6},{5,7},{6,4},{7,5},{8,10},{9,11},{10,... | collective-permute-start | bytes 3080 | tf_op jit(solution)/shard_map/ppermute | solution.py:19
  18.1 2.4 %copy-start.8 = (s32[1,256]{1,0:T(1,128)S(1)}, s32[1,256]{1,0:T(1,128)}, u32[]{:S(2)}) copy-start(s32[1,256]{1,0:T(1,128)} %param.9) | copy-start | bytes 3076
  20.3 7.8 %copy-start.9 = (s32[32]{0:T(128)S(1)}, s32[32]{0:T(128)}, u32[]{:S(2)}) copy-start(s32[32]{0:T(128)} %param.10) | copy-start | bytes 388
  20.5 26.7 %copy-start.1 = (bf16[128,4096]{1,0:T(8,128)(2,1)}, bf16[128,4096]{1,0:T(8,128)(2,1)S(1)}, u32[]{:S(2)}) copy-start(bf16[128,4096]{1,0:T(8,128)(2,1)S(1)} %get-tuple-element.44.refs_1_) | copy-start | bytes 3145732
  20.5 26.7 %copy-start.2 = (bf16[128,4096]{1,0:T(8,128)(2,1)}, bf16[128,4096]{1,0:T(8,128)(2,1)S(1)}, u32[]{:S(2)}) copy-start(bf16[128,4096]{1,0:T(8,128)(2,1)S(1)} %get-tuple-element.43.refs_0_) | copy-start | bytes 3145732
  20.5 7.3 %collective-permute-start.5 = (s32[256]{0:T(256)S(1)}, s32[256]{0:T(256)S(1)}, u32[]{:S(2)}, u32[]{:S(2)}) collective-permute-start(s32[256]{0:T(256)S(1)} %bitcast.30), channel_id=1, source_target_pairs={{0,1},{1,2},{2,3},{3,0},{4,5},{5,6},{6,7},{7,4},{8,9},{9,10},{10,1... | collective-permute-start | bytes 3080 | tf_op jit(solution)/shard_map/ppermute | solution.py:19
  28.9 27.7 %collective-permute-start.6 = (bf16[128,4096]{1,0:T(8,128)(2,1)S(1)}, bf16[128,4096]{1,0:T(8,128)(2,1)}, u32[]{:S(2)}, u32[]{:S(2)}) collective-permute-start(bf16[128,4096]{1,0:T(8,128)(2,1)S(1)} %get-tuple-element.43.refs_0_), channel_id=1, source_target_pairs={{0,1},{1,2},{2,3},{3,0},{4,5},{5,6},{6,7},{7,4},{8,9},{9,10},{10,1... | collective-permute-start | bytes 3145736 | tf_op jit(solution)/shard_map/ppermute | solution.py:19
  28.9 27.7 %collective-permute-start.7 = (bf16[128,4096]{1,0:T(8,128)(2,1)S(1)}, bf16[128,4096]{1,0:T(8,128)(2,1)}, u32[]{:S(2)}, u32[]{:S(2)}) collective-permute-start(bf16[128,4096]{1,0:T(8,128)(2,1)S(1)} %get-tuple-element.44.refs_1_), channel_id=1, source_target_pairs={{0,3},{1,0},{2,1},{3,2},{4,7},{5,4},{6,5},{7,6},{8,11},{9,8},{10,9... | collective-permute-start | bytes 3145736 | tf_op jit(solution)/shard_map/ppermute | solution.py:19
  35.4 39.6 %collective-permute-start.10 = (bf16[128,4096]{1,0:T(8,128)(2,1)S(1)}, bf16[128,4096]{1,0:T(8,128)(2,1)}, u32[]{:S(2)}, u32[]{:S(2)}) collective-permute-start(bf16[128,4096]{1,0:T(8,128)(2,1)S(1)} %get-tuple-element.43.refs_0_), channel_id=1, source_target_pairs={{0,3},{1,0},{2,1},{3,2},{4,7},{5,4},{6,5},{7,6},{8,11},{9,8},{10,9... | collective-permute-start | bytes 3145736 | tf_op jit(solution)/shard_map/ppermute | solution.py:19
  35.5 40.7 %collective-permute-start.11 = (bf16[128,4096]{1,0:T(8,128)(2,1)S(1)}, bf16[128,4096]{1,0:T(8,128)(2,1)}, u32[]{:S(2)}, u32[]{:S(2)}) collective-permute-start(bf16[128,4096]{1,0:T(8,128)(2,1)S(1)} %get-tuple-element.44.refs_1_), channel_id=1, source_target_pairs={{0,1},{1,2},{2,3},{3,0},{4,5},{5,6},{6,7},{7,4},{8,9},{9,10},{10,1... | collective-permute-start | bytes 3145736 | tf_op jit(solution)/shard_map/ppermute | solution.py:19
  56.6 42.1 %collective-permute-start.8 = (bf16[128,4096]{1,0:T(8,128)(2,1)}, bf16[128,4096]{1,0:T(8,128)(2,1)S(1)}, u32[]{:S(2)}, u32[]{:S(2)}) collective-permute-start(bf16[128,4096]{1,0:T(8,128)(2,1)} %collective-permute-done.6.refs_2_), channel_id=1, source_target_pairs={{0,1},{1,2},{2,3},{3,0},{4,5},{5,6},{6,7},{7,4},{8,9},{9,10},{10,1... | collective-permute-start | bytes 3145736 | tf_op jit(solution)/shard_map/ppermute | solution.py:19
  56.7 42.0 %collective-permute-start.9 = (bf16[128,4096]{1,0:T(8,128)(2,1)}, bf16[128,4096]{1,0:T(8,128)(2,1)}, u32[]{:S(2)}, u32[]{:S(2)}) collective-permute-start(bf16[128,4096]{1,0:T(8,128)(2,1)} %collective-permute-done.7.refs_1_), channel_id=1, source_target_pairs={{0,3},{1,0},{2,1},{3,2},{4,7},{5,4},{6,5},{7,6},{8,11},{9,8},{10,9... | collective-permute-start | bytes 3145736 | tf_op jit(solution)/shard_map/ppermute | solution.py:19
  105.9 26.9 %all-to-all-start = ((bf16[32,64,256]{2,1,0:T(8,128)(2,1)}), bf16[32,64,256]{2,1,0:T(8,128)(2,1)S(1)}, u32[]{:S(2)}, u32[]{:S(2)}) async-start(bf16[32,64,256]{2,1,0:T(8,128)(2,1)} %get-tuple-element.47), calls=%async_computation | async-start | bytes 2097152 | tf_op jit(solution)/shard_map/all_to_all | solution.py:343
  115.9 10.0 %copy-start.7 = (bf16[256,1024]{1,0:T(8,128)(2,1)S(1)}, bf16[256,1024]{1,0:T(8,128)(2,1)}, u32[]{:S(2)}) copy-start(bf16[256,1024]{1,0:T(8,128)(2,1)} %attend.3) | copy-start | bytes 1572868
  125.2 23.8 %collective-permute-start.12 = (bf16[256,1024]{1,0:T(8,128)(2,1)}, bf16[256,1024]{1,0:T(8,128)(2,1)S(1)}, u32[]{:S(2)}, u32[]{:S(2)}) collective-permute-start(bf16[256,1024]{1,0:T(8,128)(2,1)} %project_q.1), channel_id=1, source_target_pairs={{0,2},{1,3},{2,0},{3,1},{4,6},{5,7},{6,4},{7,5},{8,10},{9,11},{10,... | collective-permute-start | bytes 1572872 | tf_op jit(solution)/shard_map/ppermute | solution.py:19
  125.9 26.2 %collective-permute-start.13 = (bf16[256,1024]{1,0:T(8,128)(2,1)S(1)}, bf16[256,1024]{1,0:T(8,128)(2,1)S(1)}, u32[]{:S(2)}, u32[]{:S(2)}) collective-permute-start(bf16[256,1024]{1,0:T(8,128)(2,1)S(1)} %copy-done.7), channel_id=1, source_target_pairs={{0,1},{1,2},{2,3},{3,0},{4,5},{5,6},{6,7},{7,4},{8,9},{9,10},{10,1... | collective-permute-start | bytes 1572872 | tf_op jit(solution)/shard_map/ppermute | solution.py:19
  132.7 19.5 %collective-permute-start.14 = (bf16[256,1024]{1,0:T(8,128)(2,1)}, bf16[256,1024]{1,0:T(8,128)(2,1)S(1)}, u32[]{:S(2)}, u32[]{:S(2)}) collective-permute-start(bf16[256,1024]{1,0:T(8,128)(2,1)} %attend.5), channel_id=1, source_target_pairs={{0,3},{1,0},{2,1},{3,2},{4,7},{5,4},{6,5},{7,6},{8,11},{9,8},{10,9... | collective-permute-start | bytes 1572872 | tf_op jit(solution)/shard_map/ppermute | solution.py:19
  136.3 32.1 %all-to-all-start.1 = ((bf16[32,64,256]{2,1,0:T(8,128)(2,1)}), bf16[32,64,256]{2,1,0:T(8,128)(2,1)S(1)}, u32[]{:S(2)}, u32[]{:S(2)}) async-start(bf16[32,64,256]{2,1,0:T(8,128)(2,1)} %reorder.1), calls=%async_computation.1 | async-start | bytes 2097152 | tf_op jit(solution)/shard_map/all_to_all | solution.py:352
  149.0 3.2 %copy-start.4 = (bf16[256,1024]{1,0:T(8,128)(2,1)}, bf16[256,1024]{1,0:T(8,128)(2,1)S(1)}, u32[]{:S(2)}) copy-start(bf16[256,1024]{1,0:T(8,128)(2,1)S(1)} %collective-permute-done.12.refs_1_) | copy-start | bytes 1572868
  (4 other events, 3.7 us)
Sparse Core Ops, SparseCore 0:
  28.0 94.5 all-gather.1

commit v3 on v2

--- a/solution.py
+++ b/solution.py
@@ -10,7 +10,7 @@
 
 HD = 128
 VMEM_LIMIT = 60 << 20
-PROJECT_WEIGHT = 1
+PROJECT_WEIGHT = 50
 LAST_WEIGHT = 120
 
 
@@ -400,7 +400,7 @@
 
     normed = normalised(tokens[0], norm_gain)
     low, high = normed[:half], normed[half:]
-    shares, low, high, ids = lax.optimization_barrier((shares, low, high, ids))
+    shares, ids, _ = lax.optimization_barrier((shares, ids, (low, high)))
     others = lax.all_gather(shares, "dp", axis=1, tiled=True)
     before_low, after_high = shifted(low, "ctx", 1), shifted(high, "ctx", -1)
     halves = [tuple((q, h) for h in (0, 1)) for q in (0, 1, 3, 2)]

time: 177 us -> 177 us (level)
  waiting for transfers between devices: 31.3 us -> 37.3 us
  starting transfers between devices: 37.5 us -> 33.2 us
  other arithmetic: 13.5 us -> 10.4 us
    all_to_all x1, waiting for transfers between devices: 0.13 us -> 7.98 us  [routed(): scattered = lax.all_to_all(pieces, 'dp', 0, 0, tiled=False)]
    all_to_all x1, starting transfers between devices: 9.35 us -> 5.91 us  [routed(): return lax.all_to_all(ordered, 'dp', 0, 0, tiled=False)]
    ppermute x15, waiting for transfers between devices: 31.1 us -> 29.3 us  [shifted(): lax.ppermute(value, axis, [(i, (i + by) % count) for i in range(count)])]
  transfers between devices with their start and end apart: 18 -> 18, of which waited for: 7 -> 6; matrix products, arithmetic and copies ran while one was open for 9% -> 8% of each run, Pallas kernels for 38% -> 39%
where the time goes in v3:
time: 177 us; the launch traced here: 176 us
  Pallas kernels  69.8 us (39%)
  waiting for transfers between devices  37.3 us (21%)
  starting transfers between devices  33.2 us (19%)
  between operations  19 us (11%)
  other arithmetic  10.4 us (6%)
  local copies, waits for them, and re-layouts  6.22 us (4%)
    pallas_call x4, Pallas kernels, project(): pl.pallas_call(functools.partial(project_kernel, part, plan), grid=(1,),...  39.2 us
    ppermute x15, waiting for transfers between devices, shifted(): lax.ppermute(value, axis, [(i, (i + by) % count) for i in range(count)])  29.3 us
    ppermute x15, starting transfers between devices, shifted(): lax.ppermute(value, axis, [(i, (i + by) % count) for i in range(count)])  17.8 us
    pallas_call x1, Pallas kernels, out_terms(): pl.pallas_call(functools.partial(out_kernel, order), grid=(1,), in_specs=...  15.3 us
    pallas_call x3, Pallas kernels, attend(): pl.pallas_call(functools.partial(attend_kernel, plan, lots), grid=(1,), i...  11.7 us
    all_to_all x1, starting transfers between devices, routed(): scattered = lax.all_to_all(pieces, 'dp', 0, 0, tiled=False)  9.52 us
    all_to_all x1, waiting for transfers between devices, routed(): scattered = lax.all_to_all(pieces, 'dp', 0, 0, tiled=False)  7.98 us
    all_to_all x1, starting transfers between devices, routed(): return lax.all_to_all(ordered, 'dp', 0, 0, tiled=False)  5.91 us
  transfers between devices with their start and end apart: 18, of which 6 were waited for; matrix products, arithmetic and copies ran while one was open for 8% of the time, Pallas kernels for 39%

profile of v3, /device:TPU:1, one launch (start us, length us, event | category | flops | bytes accessed | tf_op | source)
XLA Modules:
  0.0 176.0 jit_solution(11872453080119159943)
XLA Ops:
  8.3 3.4 %collective-permute-start.2 = (bf16[32,4096]{1,0:T(8,128)(2,1)S(1)}, bf16[32,4096]{1,0:T(8,128)(2,1)S(1)}, u32[]{:S(2)}, u32[]{:S(2)}) collective-permute-start(bf16[32,4096]{1,0:T(8,128)(2,1)S(1)} %constant_dynamic-slice_fusion), channel_id=1, source_target_pairs={{0,3},{1,0},{2,1},{3,2},{4,7},{5,4},{6,5},{7,6},{8,11},{9,8},{10,9... | collective-permute-start | bytes 786440 | tf_op jit(solution)/shard_map/ppermute | solution.py:19
  12.8 2.1 %collective-permute-start.3 = (s32[256]{0:T(256)}, s32[256]{0:T(256)S(1)}, u32[]{:S(2)}, u32[]{:S(2)}) collective-permute-start(s32[256]{0:T(256)} %bitcast.28), channel_id=1, source_target_pairs={{0,3},{1,0},{2,1},{3,2},{4,7},{5,4},{6,5},{7,6},{8,11},{9,8},{10,9... | collective-permute-start | bytes 3080 | tf_op jit(solution)/shard_map/ppermute | solution.py:19
  16.3 2.1 %fusion = f32[256]{0:T(256)S(1)} fusion(bf16[1,256,4096]{2,1,0:T(8,128)(2,1)} %param.8), kind=kLoop, calls=%fused_computation.2 | loop fusion | flops 3145472 | bytes 2098176 | tf_op jit(solution)/shard_map/reduce_sum | solution.py:24
  18.4 1.5 fusion.2
  22.0 2.2 %collective-permute-start.6 = (bf16[128,4096]{1,0:T(8,128)(2,1)}, bf16[128,4096]{1,0:T(8,128)(2,1)}, u32[]{:S(2)}, u32[]{:S(2)}) collective-permute-start(bf16[128,4096]{1,0:T(8,128)(2,1)} %get-tuple-element.39.refs_0_), channel_id=1, source_target_pairs={{0,1},{1,2},{2,3},{3,0},{4,5},{5,6},{6,7},{7,4},{8,9},{9,10},{10,1... | collective-permute-start | bytes 3145736 | tf_op jit(solution)/shard_map/ppermute | solution.py:19
  24.2 2.9 %collective-permute-done = bf16[32,4096]{1,0:T(8,128)(2,1)S(1)} collective-permute-done((bf16[32,4096]{1,0:T(8,128)(2,1)S(1)}, bf16[32,4096]{1,0:T(8,128)(2,1)S(1)}, u32[]{:S(2)}, u32[]{:S(2)}) %collective-permute-start) | collective-permute-done | bytes 262176 | tf_op jit(solution)/shard_map/ppermute | solution.py:19
  34.0 1.9 %fusion.3 = (f32[1024,64]{1,0:T(8,128)S(1)}, f32[1024,64]{1,0:T(8,128)S(1)}, f32[1024,64]{1,0:T(8,128)S(1)}) fusion(f32[64]{0:T(128)S(1)} %multiply_power_fusion, f32[1024]{0:T(1024)S(1)} %subtract_convert_fusion), kind=kLoop, calls=%fused_computation.11 | loop fusion | flops 131072 | bytes 790784 | tf_op jit(solution)/shard_map/neg | solution.py:35
  41.0 9.2 %project_all.2.refs_2_.refs_4_.refs_7_.refs_5_.refs_9_ = bf16[6,256,256]{2,1,0:T(8,128)(2,1)} custom-call(bf16[128,4096]{1,0:T(8,128)(2,1)} %get-tuple-element.39.refs_0_, bf16[128,4096]{1,0:T(8,128)(2,1)} %get-tuple-element.40.refs_1_, f32[1024,128]{1,0:T(8,128)} %get-tuple-element.32.refs_2_.refs_4_, f32[1024,128]{1,0:T(8,128)} %get-tuple-element.33.refs_3_.refs_5_, ...), custom_call_target="tpu_custom_call" | custom-call | flops 161061273600 | bytes 14680064 | tf_op jit(solution)/shard_map/project_all/pallas_call | solution.py:146
  51.8 2.5 %collective-permute-start.9 = (bf16[128,4096]{1,0:T(8,128)(2,1)}, bf16[128,4096]{1,0:T(8,128)(2,1)}, u32[]{:S(2)}, u32[]{:S(2)}) collective-permute-start(bf16[128,4096]{1,0:T(8,128)(2,1)} %collective-permute-done.7.refs_1_), channel_id=1, source_target_pairs={{0,3},{1,0},{2,1},{3,2},{4,7},{5,4},{6,5},{7,6},{8,11},{9,8},{10,9... | collective-permute-start | bytes 3145736 | tf_op jit(solution)/shard_map/ppermute | solution.py:19
  54.3 19.8 %collective-permute-done.10.refs_0_ = bf16[128,4096]{1,0:T(8,128)(2,1)} collective-permute-done((bf16[128,4096]{1,0:T(8,128)(2,1)}, bf16[128,4096]{1,0:T(8,128)(2,1)}, u32[]{:S(2)}, u32[]{:S(2)}) %collective-permute-start.10) | collective-permute-done | bytes 1048608 | tf_op jit(solution)/shard_map/ppermute | solution.py:19
  74.1 13.0 %project_all.3.refs_3_.refs_5_.refs_8_.refs_10_ = bf16[6,512,256]{2,1,0:T(8,128)(2,1)} custom-call(bf16[128,4096]{1,0:T(8,128)(2,1)} %collective-permute-done.10.refs_0_, bf16[128,4096]{1,0:T(8,128)(2,1)} %collective-permute-done.7.refs_1_, bf16[128,4096]{1,0:T(8,128)(2,1)} %collective-permute-done.6.refs_2_, ...), custom_call_target="tpu_custom_call" | custom-call | flops 322122547200 | bytes 16777216 | tf_op jit(solution)/shard_map/project_all/pallas_call | solution.py:146
  87.1 4.2 %attend.3 = bf16[256,1024]{1,0:T(8,128)(2,1)} custom-call(s32[2]{0:T(128)} %get-tuple-element.36.refs_0_, s32[1024,128]{1,0:T(8,128)} %broadcast_in_dim.48.refs_1_.refs_8_, bf16[6,256,256]{2,1,0:T(8,128)(2,1)} %project_all.2.refs_2_.refs_4_.refs_7_.refs_5_.refs_9_, bf16[6,512,256]{2,1,0:T(8,128)(2,1)} %project_all.3.refs_3_.refs_5_.refs_8_.refs_10_, ...), custom_call_target="tpu_custom_call" | custom-call | tf_op jit(solution)/shard_map/attend/pallas_call | solution.py:244
  91.3 1.7 collective-permute-done.8.refs_0_
  93.0 3.5 %collective-permute-done.9.refs_1_ = bf16[128,4096]{1,0:T(8,128)(2,1)} collective-permute-done((bf16[128,4096]{1,0:T(8,128)(2,1)}, bf16[128,4096]{1,0:T(8,128)(2,1)}, u32[]{:S(2)}, u32[]{:S(2)}) %collective-permute-start.9) | collective-permute-done | bytes 1048608 | tf_op jit(solution)/shard_map/ppermute | solution.py:19
  96.6 6.2 %project_kv.1 = (bf16[2,256,256]{2,1,0:T(8,128)(2,1)}, bf16[32,64,256]{2,1,0:T(8,128)(2,1)}) custom-call(bf16[128,4096]{1,0:T(8,128)(2,1)} %collective-permute-done.8.refs_0_, bf16[128,4096]{1,0:T(8,128)(2,1)} %collective-permute-done.9.refs_1_, f32[1024,128]{1,0:T(8,128)} %get-tuple-element.32.refs_2_.refs_4_, ...), custom_call_target="tpu_custom_call" | custom-call | flops 128849018880 | bytes 6291456 | tf_op jit(solution)/shard_map/project_kv/pallas_call | solution.py:146
  102.8 9.5 %all-to-all-start = ((bf16[32,64,256]{2,1,0:T(8,128)(2,1)}), bf16[32,64,256]{2,1,0:T(8,128)(2,1)S(1)}, u32[]{:S(2)}, u32[]{:S(2)}) async-start(bf16[32,64,256]{2,1,0:T(8,128)(2,1)} %get-tuple-element.43), calls=%async_computation | async-start | bytes 2097152 | tf_op jit(solution)/shard_map/all_to_all | solution.py:343
  112.3 10.7 %project_q.1 = bf16[256,1024]{1,0:T(8,128)(2,1)} custom-call(bf16[128,4096]{1,0:T(8,128)(2,1)} %collective-permute-done.8.refs_0_, bf16[128,4096]{1,0:T(8,128)(2,1)} %collective-permute-done.9.refs_1_, f32[1024,128]{1,0:T(8,128)} %get-tuple-element.32.refs_2_.refs_4_, f32[1024,128]{1,0:T(8,128)} %get-tuple-element.33.refs_3_.refs_5_, ...), custom_call_target="tpu_custom_call" | custom-call | bytes 10485760 | tf_op jit(solution)/shard_map/project_q/pallas_call | solution.py:146
  124.4 4.2 %attend.5 = bf16[256,1024]{1,0:T(8,128)(2,1)} custom-call(s32[2]{0:T(128)} %get-tuple-element.48.refs_0_, s32[1024,128]{1,0:T(8,128)} %broadcast_in_dim.48.refs_1_.refs_8_, bf16[6,256,256]{2,1,0:T(8,128)(2,1)} %project_all.2.refs_2_.refs_4_.refs_7_.refs_5_.refs_9_, bf16[6,512,256]{2,1,0:T(8,128)(2,1)} %project_all.3.refs_3_.refs_5_.refs_8_.refs_10_, ...), custom_call_target="tpu_custom_call" | custom-call | tf_op jit(solution)/shard_map/attend/pallas_call | solution.py:244
  128.6 2.3 %collective-permute-start.14 = (bf16[256,1024]{1,0:T(8,128)(2,1)}, bf16[256,1024]{1,0:T(8,128)(2,1)S(1)}, u32[]{:S(2)}, u32[]{:S(2)}) collective-permute-start(bf16[256,1024]{1,0:T(8,128)(2,1)} %attend.5), channel_id=1, source_target_pairs={{0,3},{1,0},{2,1},{3,2},{4,7},{5,4},{6,5},{7,6},{8,11},{9,8},{10,9... | collective-permute-start | bytes 1572872 | tf_op jit(solution)/shard_map/ppermute | solution.py:19
  130.9 8.0 %all-to-all-done.in_ref = bf16[32,64,256]{2,1,0:T(8,128)(2,1)S(1)} async-done(((bf16[32,64,256]{2,1,0:T(8,128)(2,1)}), bf16[32,64,256]{2,1,0:T(8,128)(2,1)S(1)}, u32[]{:S(2)}, u32[]{:S(2)}) %all-to-all-start) | async-done | bytes 1048608 | tf_op jit(solution)/shard_map/all_to_all | solution.py:343
  139.8 2.5 %reorder.1 = bf16[32,64,256]{2,1,0:T(8,128)(2,1)} custom-call(s32[32]{0:T(128)} %select_reduce_fusion.1.source_ref, bf16[32,64,256]{2,1,0:T(8,128)(2,1)} %copy-done.1), custom_call_target="tpu_custom_call" | custom-call | tf_op jit(solution)/shard_map/reorder/pallas_call | solution.py:344
  142.3 5.9 %all-to-all-start.1 = ((bf16[32,64,256]{2,1,0:T(8,128)(2,1)}), bf16[32,64,256]{2,1,0:T(8,128)(2,1)S(1)}, u32[]{:S(2)}, u32[]{:S(2)}) async-start(bf16[32,64,256]{2,1,0:T(8,128)(2,1)} %reorder.1), calls=%async_computation.1 | async-start | bytes 2097152 | tf_op jit(solution)/shard_map/all_to_all | solution.py:352
  148.3 3.3 %attend.4.refs_0_ = bf16[256,1024]{1,0:T(8,128)(2,1)} custom-call(s32[2]{0:T(128)} %get-tuple-element.44.refs_0_, s32[1024,128]{1,0:T(8,128)} %broadcast_in_dim.48.refs_1_.refs_8_, bf16[6,256,256]{2,1,0:T(8,128)(2,1)} %project_all.2.refs_2_.refs_4_.refs_7_.refs_5_.refs_9_, bf16[6,512,256]{2,1,0:T(8,128)(2,1)} %project_all.3.refs_3_.refs_5_.refs_8_.refs_10_, ...), custom_call_target="tpu_custom_call" | custom-call | tf_op jit(solution)/shard_map/attend/pallas_call | solution.py:244
  152.7 15.3 %out_terms.1 = bf16[256,4096]{1,0:T(8,128)(2,1)} custom-call(bf16[256,1024]{1,0:T(8,128)(2,1)} %attend.4.refs_0_, bf16[256,1024]{1,0:T(8,128)(2,1)} %copy-done.2, bf16[256,1024]{1,0:T(8,128)(2,1)} %copy-done.3, bf16[256,1024]{1,0:T(8,128)(2,1)} %copy-done.4, bf16[1024,4096]{1,0:T(8,128)(2,1)} %refs_4_.7, ...), custom_call_target="tpu_custom_call" | custom-call | flops 8589934592 | bytes 33554432 | tf_op jit(solution)/shard_map/out_terms/pallas_call | solution.py:312
  (69 shorter events, 19.1 us)
Async XLA Ops:
  7.2 11.2 %copy-start = (bf16[1,256,4096]{2,1,0:T(8,128)(2,1)S(1)}, bf16[1,256,4096]{2,1,0:T(8,128)(2,1)}, u32[]{:S(2)}) copy-start(bf16[1,256,4096]{2,1,0:T(8,128)(2,1)} %param.8) | copy-start | bytes 6291460
  7.2 144.5 %all-gather.2.cloned.1.call-start = ((), (), s32[]{:S(2)}) async-start(), calls=%async_computation.2 | async-start | bytes 25952256 | tf_op jit(solution)/shard_map/all_gather | solution.py:404
  8.3 13.6 %collective-permute-start.2 = (bf16[32,4096]{1,0:T(8,128)(2,1)S(1)}, bf16[32,4096]{1,0:T(8,128)(2,1)S(1)}, u32[]{:S(2)}, u32[]{:S(2)}) collective-permute-start(bf16[32,4096]{1,0:T(8,128)(2,1)S(1)} %constant_dynamic-slice_fusion), channel_id=1, source_target_pairs={{0,3},{1,0},{2,1},{3,2},{4,7},{5,4},{6,5},{7,6},{8,11},{9,8},{10,9... | collective-permute-start | bytes 786440 | tf_op jit(solution)/shard_map/ppermute | solution.py:19
  11.7 10.3 %collective-permute-start.1 = (bf16[32,4096]{1,0:T(8,128)(2,1)S(1)}, bf16[32,4096]{1,0:T(8,128)(2,1)S(1)}, u32[]{:S(2)}, u32[]{:S(2)}) collective-permute-start(bf16[32,4096]{1,0:T(8,128)(2,1)S(1)} %constant_dynamic-slice_fusion), channel_id=1, source_target_pairs={{0,2},{1,3},{2,0},{3,1},{4,6},{5,7},{6,4},{7,5},{8,10},{9,11},{10,... | collective-permute-start | bytes 786440 | tf_op jit(solution)/shard_map/ppermute | solution.py:19
  12.2 14.8 %collective-permute-start = (bf16[32,4096]{1,0:T(8,128)(2,1)S(1)}, bf16[32,4096]{1,0:T(8,128)(2,1)S(1)}, u32[]{:S(2)}, u32[]{:S(2)}) collective-permute-start(bf16[32,4096]{1,0:T(8,128)(2,1)S(1)} %constant_dynamic-slice_fusion), channel_id=1, source_target_pairs={{0,1},{1,2},{2,3},{3,0},{4,5},{5,6},{6,7},{7,4},{8,9},{9,10},{10,1... | collective-permute-start | bytes 786440 | tf_op jit(solution)/shard_map/ppermute | solution.py:19
  12.8 15.2 %collective-permute-start.3 = (s32[256]{0:T(256)}, s32[256]{0:T(256)S(1)}, u32[]{:S(2)}, u32[]{:S(2)}) collective-permute-start(s32[256]{0:T(256)} %bitcast.28), channel_id=1, source_target_pairs={{0,3},{1,0},{2,1},{3,2},{4,7},{5,4},{6,5},{7,6},{8,11},{9,8},{10,9... | collective-permute-start | bytes 3080 | tf_op jit(solution)/shard_map/ppermute | solution.py:19
  14.9 13.2 %collective-permute-start.4 = (s32[256]{0:T(256)}, s32[256]{0:T(256)S(1)}, u32[]{:S(2)}, u32[]{:S(2)}) collective-permute-start(s32[256]{0:T(256)} %bitcast.29), channel_id=1, source_target_pairs={{0,2},{1,3},{2,0},{3,1},{4,6},{5,7},{6,4},{7,5},{8,10},{9,11},{10,... | collective-permute-start | bytes 3080 | tf_op jit(solution)/shard_map/ppermute | solution.py:19
  18.4 3.0 %copy-start.7 = (s32[32]{0:T(128)S(1)}, s32[32]{0:T(128)}, u32[]{:S(2)}) copy-start(s32[32]{0:T(128)} %param.10) | copy-start | bytes 388
  18.4 3.6 %copy-start.6 = (s32[1,256]{1,0:T(1,128)S(1)}, s32[1,256]{1,0:T(1,128)}, u32[]{:S(2)}) copy-start(s32[1,256]{1,0:T(1,128)} %param.9) | copy-start | bytes 3076
  22.0 6.1 %collective-permute-start.5 = (s32[256]{0:T(256)S(1)}, s32[256]{0:T(256)S(1)}, u32[]{:S(2)}, u32[]{:S(2)}) collective-permute-start(s32[256]{0:T(256)S(1)} %bitcast.30), channel_id=1, source_target_pairs={{0,1},{1,2},{2,3},{3,0},{4,5},{5,6},{6,7},{7,4},{8,9},{9,10},{10,1... | collective-permute-start | bytes 3080 | tf_op jit(solution)/shard_map/ppermute | solution.py:19
  22.0 28.2 %collective-permute-start.6 = (bf16[128,4096]{1,0:T(8,128)(2,1)}, bf16[128,4096]{1,0:T(8,128)(2,1)}, u32[]{:S(2)}, u32[]{:S(2)}) collective-permute-start(bf16[128,4096]{1,0:T(8,128)(2,1)} %get-tuple-element.39.refs_0_), channel_id=1, source_target_pairs={{0,1},{1,2},{2,3},{3,0},{4,5},{5,6},{6,7},{7,4},{8,9},{9,10},{10,1... | collective-permute-start | bytes 3145736 | tf_op jit(solution)/shard_map/ppermute | solution.py:19
  27.1 24.5 %collective-permute-start.7 = (bf16[128,4096]{1,0:T(8,128)(2,1)}, bf16[128,4096]{1,0:T(8,128)(2,1)}, u32[]{:S(2)}, u32[]{:S(2)}) collective-permute-start(bf16[128,4096]{1,0:T(8,128)(2,1)} %get-tuple-element.40.refs_1_), channel_id=1, source_target_pairs={{0,3},{1,0},{2,1},{3,2},{4,7},{5,4},{6,5},{7,6},{8,11},{9,8},{10,9... | collective-permute-start | bytes 3145736 | tf_op jit(solution)/shard_map/ppermute | solution.py:19
  39.5 34.6 %collective-permute-start.10 = (bf16[128,4096]{1,0:T(8,128)(2,1)}, bf16[128,4096]{1,0:T(8,128)(2,1)}, u32[]{:S(2)}, u32[]{:S(2)}) collective-permute-start(bf16[128,4096]{1,0:T(8,128)(2,1)} %get-tuple-element.39.refs_0_), channel_id=1, source_target_pairs={{0,3},{1,0},{2,1},{3,2},{4,7},{5,4},{6,5},{7,6},{8,11},{9,8},{10,9... | collective-permute-start | bytes 3145736 | tf_op jit(solution)/shard_map/ppermute | solution.py:19
  40.3 33.8 %collective-permute-start.11 = (bf16[128,4096]{1,0:T(8,128)(2,1)}, bf16[128,4096]{1,0:T(8,128)(2,1)}, u32[]{:S(2)}, u32[]{:S(2)}) collective-permute-start(bf16[128,4096]{1,0:T(8,128)(2,1)} %get-tuple-element.40.refs_1_), channel_id=1, source_target_pairs={{0,1},{1,2},{2,3},{3,0},{4,5},{5,6},{6,7},{7,4},{8,9},{9,10},{10,1... | collective-permute-start | bytes 3145736 | tf_op jit(solution)/shard_map/ppermute | solution.py:19
  51.6 41.4 %collective-permute-start.8 = (bf16[128,4096]{1,0:T(8,128)(2,1)}, bf16[128,4096]{1,0:T(8,128)(2,1)}, u32[]{:S(2)}, u32[]{:S(2)}) collective-permute-start(bf16[128,4096]{1,0:T(8,128)(2,1)} %collective-permute-done.6.refs_2_), channel_id=1, source_target_pairs={{0,1},{1,2},{2,3},{3,0},{4,5},{5,6},{6,7},{7,4},{8,9},{9,10},{10,1... | collective-permute-start | bytes 3145736 | tf_op jit(solution)/shard_map/ppermute | solution.py:19
  51.8 44.8 %collective-permute-start.9 = (bf16[128,4096]{1,0:T(8,128)(2,1)}, bf16[128,4096]{1,0:T(8,128)(2,1)}, u32[]{:S(2)}, u32[]{:S(2)}) collective-permute-start(bf16[128,4096]{1,0:T(8,128)(2,1)} %collective-permute-done.7.refs_1_), channel_id=1, source_target_pairs={{0,3},{1,0},{2,1},{3,2},{4,7},{5,4},{6,5},{7,6},{8,11},{9,8},{10,9... | collective-permute-start | bytes 3145736 | tf_op jit(solution)/shard_map/ppermute | solution.py:19
  102.8 36.0 %all-to-all-start = ((bf16[32,64,256]{2,1,0:T(8,128)(2,1)}), bf16[32,64,256]{2,1,0:T(8,128)(2,1)S(1)}, u32[]{:S(2)}, u32[]{:S(2)}) async-start(bf16[32,64,256]{2,1,0:T(8,128)(2,1)} %get-tuple-element.43), calls=%async_computation | async-start | bytes 2097152 | tf_op jit(solution)/shard_map/all_to_all | solution.py:343
  112.3 10.8 %copy-start.5 = (bf16[256,1024]{1,0:T(8,128)(2,1)S(1)}, bf16[256,1024]{1,0:T(8,128)(2,1)}, u32[]{:S(2)}) copy-start(bf16[256,1024]{1,0:T(8,128)(2,1)} %attend.3) | copy-start | bytes 1572868
  123.0 28.5 %collective-permute-start.12 = (bf16[256,1024]{1,0:T(8,128)(2,1)}, bf16[256,1024]{1,0:T(8,128)(2,1)S(1)}, u32[]{:S(2)}, u32[]{:S(2)}) collective-permute-start(bf16[256,1024]{1,0:T(8,128)(2,1)} %project_q.1), channel_id=1, source_target_pairs={{0,2},{1,3},{2,0},{3,1},{4,6},{5,7},{6,4},{7,5},{8,10},{9,11},{10,... | collective-permute-start | bytes 1572872 | tf_op jit(solution)/shard_map/ppermute | solution.py:19
  123.1 28.5 %collective-permute-start.13 = (bf16[256,1024]{1,0:T(8,128)(2,1)S(1)}, bf16[256,1024]{1,0:T(8,128)(2,1)S(1)}, u32[]{:S(2)}, u32[]{:S(2)}) collective-permute-start(bf16[256,1024]{1,0:T(8,128)(2,1)S(1)} %copy-done.5), channel_id=1, source_target_pairs={{0,1},{1,2},{2,3},{3,0},{4,5},{5,6},{6,7},{7,4},{8,9},{9,10},{10,1... | collective-permute-start | bytes 1572872 | tf_op jit(solution)/shard_map/ppermute | solution.py:19
  128.6 23.0 %collective-permute-start.14 = (bf16[256,1024]{1,0:T(8,128)(2,1)}, bf16[256,1024]{1,0:T(8,128)(2,1)S(1)}, u32[]{:S(2)}, u32[]{:S(2)}) collective-permute-start(bf16[256,1024]{1,0:T(8,128)(2,1)} %attend.5), channel_id=1, source_target_pairs={{0,3},{1,0},{2,1},{3,2},{4,7},{5,4},{6,5},{7,6},{8,11},{9,8},{10,9... | collective-permute-start | bytes 1572872 | tf_op jit(solution)/shard_map/ppermute | solution.py:19
  142.3 25.7 %all-to-all-start.1 = ((bf16[32,64,256]{2,1,0:T(8,128)(2,1)}), bf16[32,64,256]{2,1,0:T(8,128)(2,1)S(1)}, u32[]{:S(2)}, u32[]{:S(2)}) async-start(bf16[32,64,256]{2,1,0:T(8,128)(2,1)} %reorder.1), calls=%async_computation.1 | async-start | bytes 2097152 | tf_op jit(solution)/shard_map/all_to_all | solution.py:352
  151.6 1.0 copy-start.3
  151.6 1.1 copy-start.4
  (2 other events, 1.8 us)
Sparse Core Ops, SparseCore 0:
  41.1 107.4 all-gather.1
